TPU v7x, 512 devices: a whole 4x4x16 slice. The times are simulated.
512 devices in a mesh: tm: 4 (over x), height: 8 (over z_lo, core), chan: 16 (over z_hi, y).
Axes of the slice: x: 4, y: 4, z: 16 (z_hi: 4, z_lo: 4; z = z_hi * 4 + z_lo), core: 2. Of those that a mesh axis runs over, the one named last changes fastest.
Arguments:
- features: bfloat16 [384, 8, 32, 160], P('chan', 'tm', 'height'), may hold values from -400 to 400, as said below
- cotangent: bfloat16 [384, 8, 32, 160], P('chan', 'tm', 'height'), may hold values from -6 to 6
- conv_weight: bfloat16 [384, 27, 384], P('chan'), may hold values from -0.0625 to 0.0625
- norm_gain: float32 [384], replicated, may hold values from 0.5 to 1.5
- norm_bias: float32 [384], replicated, may hold values from -3 to 3
Outputs:
- input_grad: bfloat16 [384, 8, 32, 160], P('chan', 'tm', 'height')
- weight_grad: float32 [384, 27, 384], P('chan')
Inputs may be any that keep to these rules, and one draw needn't show every extreme that they name: `features`: bounded activations.
All inputs are finite; a program needn't handle non-finite values.
Results may differ from a plain program's by a relative error of at most 0.003.
Values may be sent and summed in bfloat16 or wider, within the bound.
A program may use at most 64 MiB of HBM per device.

v0:
```python
import math

import jax
import jax.numpy as jnp
from jax import lax
from jax.sharding import PartitionSpec as P


def from_behind(block, axis, distance):
    devices = range(lax.axis_size(axis))
    route = [(i - distance, i) for i in devices if i - distance in devices]
    return lax.ppermute(block, axis, route)


def with_halo(array, sides, width):
    for axis, dim in sides:
        size, length = (lax.axis_size(axis), array.shape[dim])
        up = [(i, (i + 1) % size) for i in range(size - 1)]
        down = [(j, i) for i, j in up]
        last = lax.slice_in_dim(array, length - width, length, axis=dim)
        first = lax.slice_in_dim(array, 0, width, axis=dim)
        before = lax.ppermute(last, axis, up)
        after = lax.ppermute(first, axis, down)
        array = jnp.concatenate([before, array, after], axis=dim)
    return array


def on_device(features, cotangent, conv_weight, norm_gain, norm_bias):
    chans, frames, rows, cols = features.shape
    whole_x = lax.all_gather(features, "chan", axis=0, tiled=True)
    total = whole_x.shape[0]
    flat_x = whole_x.reshape(total, -1).astype(jnp.float32)
    inv_rms = lax.rsqrt(jnp.mean(flat_x * flat_x, axis=0, keepdims=True) + 1e-06)
    normed = flat_x * inv_rms * norm_gain[:, None] + norm_bias[:, None]
    active = jax.nn.silu(normed).astype(jnp.bfloat16)
    ahead = from_behind(cotangent, "tm", -1)
    longer = jnp.concatenate([cotangent, ahead], axis=1)
    bordered = with_halo(longer, (("height", 2),), 1)
    padded = jnp.pad(bordered, ((0, 0), (0, 0), (0, 0), (1, 1)))
    taps = []
    for kt in range(3):
        for kh in range(3):
            for kw in range(3):
                taps.append(
                    padded[
                        :, 2 - kt : 2 - kt + frames, 2 - kh : 2 - kh + rows, 2 - kw : 2 - kw + cols
                    ]
                )
    stacked = jnp.stack(taps, axis=1).reshape(chans * 27, -1)
    local_sums = lax.dot_general(
        stacked, active, (((1,), (1,)), ((), ())), preferred_element_type=jnp.float32
    )
    positions = frames * lax.axis_size("tm") * rows * lax.axis_size("height") * cols
    summed = lax.psum(local_sums, ("tm", "height"))
    weight_grad = (summed / math.sqrt(positions)).reshape(chans, 27, total)
    sig = jax.nn.sigmoid(normed)
    slope = sig * (1.0 + normed * (1.0 - sig))
    offset = lax.axis_index("chan") * chans
    weight_flat = conv_weight.reshape(chans * 27, total)
    partial_value = lax.dot_general(
        weight_flat, stacked, (((0,), (0,)), ((), ())), preferred_element_type=jnp.float32
    )
    act_grad = lax.psum(partial_value, "chan")
    upstream = act_grad * slope * norm_gain[:, None]
    dots = jnp.sum(upstream * flat_x, axis=0, keepdims=True)
    back = inv_rms * upstream - flat_x * inv_rms**3 * dots / total
    own_back = lax.dynamic_slice_in_dim(back, offset, chans, 0)
    result = cotangent.reshape(chans, -1).astype(jnp.float32) + own_back
    return (result.astype(jnp.bfloat16).reshape(features.shape), weight_grad)


def solution(mesh):
    return jax.shard_map(
        on_device,
        mesh=mesh,
        in_specs=(
            P("chan", "tm", "height", None),
            P("chan", "tm", "height", None),
            P("chan", None, None),
            P(),
            P(),
        ),
        out_specs=(P("chan", "tm", "height", None), P("chan", None, None)),
        check_vma=False,
    )
```

profile of v0, /device:TPU:1, one launch (start us, length us, event | category | flops | bytes accessed | tf_op | source)
XLA Modules:
  0.0 685.4 jit_solution(8743268547803639951)
XLA Ops:
  7.2 1.3 collective-permute-start
  8.5 91.9 %all_gather.3 = bf16[384,2,4,160]{3,2,1,0:T(4,128)(2,1)S(1)} all-gather(bf16[24,2,4,160]{3,2,1,0:T(4,128)(2,1)} %param.5), channel_id=1, replica_groups=mesh['tm'=4,'height'=8,'chan'=16] {'chan'}, dimensions={0}, use_global_device_ids=true | all-gather | bytes 1044480 | tf_op jit(solution)/shard_map/all_gather | solution.py:30
  100.5 1.4 copy.18
  101.9 0.4 multiply_reduce_fusion.1
  102.4 0.1 fusion.38
  102.6 6.5 collective-permute-start.1
  109.1 1.9 collective-permute-start.2
  111.0 1.7 multiply_convert_fusion
  112.7 2.3 collective-permute-done.2
  115.0 0.8 fusion.10
  115.8 0.1 fusion.37
  115.9 0.2 fusion.36
  116.1 0.1 fusion.35
  116.2 0.2 fusion.34
  116.4 0.1 fusion.33
  116.5 0.1 fusion.32
  116.6 0.1 fusion.31
  116.8 0.2 fusion.29
  117.0 0.2 fusion.28
  117.2 0.2 fusion.26
  117.4 0.1 fusion.24
  117.5 0.1 fusion.23
  117.6 0.1 fusion.22
  117.8 0.2 fusion.20
  118.0 0.2 fusion.19
  118.2 0.1 fusion.17
  118.2 0.2 fusion.16
  118.5 0.1 fusion.15
  118.5 0.1 fusion.14
  118.7 0.1 fusion.13
  118.9 2.4 copy.19
  121.3 5.5 reshape.64
  126.8 3.2 fusion.39
  130.0 0.2 all-reduce.4.cloned.1.call-start
  130.2 1.1 copy.20
  131.3 1.0 reshape.65
  132.3 3.6 convolution_bitcast_fusion
  135.9 0.1 rsqrt.16
  135.9 1.0 copy.17
  137.0 1.5 bitcast_convert_fusion
  138.5 273.8 %all-reduce.6.cloned.1.call-done = f32[648,384]{1,0:T(8,128)} async-done(((f32[648,384]{1,0:T(8,128)}), f32[648,384]{1,0:T(8,128)}) %all-reduce.6.cloned.1.call-update) | async-done | bytes 995344 | tf_op jit(solution)/shard_map/psum | solution.py:54
  412.3 1.3 broadcast_multiply_fusion
  413.6 0.1 reshape.67
  413.7 1.5 copy.22
  415.2 257.2 %all-reduce.4.cloned.1.call-done = f32[384,1280]{0,1:T(8,128)} async-done(((f32[384,1280]{0,1:T(8,128)}), f32[384,1280]{0,1:T(8,128)}) %all-reduce.4.cloned.1.call-update) | async-done | bytes 1966096 | tf_op jit(solution)/shard_map/psum | solution.py:63
  672.5 3.0 multiply_reduce_fusion
  675.4 2.2 fusion.3
  677.7 0.8 copy.21
  (24 shorter events, 0.5 us)
Async XLA Ops:
  7.2 95.1 %copy-start.1 = (bf16[24,2,4,160]{3,2,1,0:T(4,128)(2,1)S(1)}, bf16[24,2,4,160]{3,2,1,0:T(4,128)(2,1)}, u32[]{:S(2)}) copy-start(bf16[24,2,4,160]{3,2,1,0:T(4,128)(2,1)} %param.6) | copy-start | bytes 184324
  7.2 103.8 %copy-start.3 = (f32[384]{0:T(512)S(1)}, f32[384]{0:T(512)}, u32[]{:S(2)}) copy-start(f32[384]{0:T(512)} %param.8) | copy-start | bytes 4612
  7.2 103.8 %copy-start.2 = (f32[384]{0:T(512)S(1)}, f32[384]{0:T(512)}, u32[]{:S(2)}) copy-start(f32[384]{0:T(512)} %param.9) | copy-start | bytes 4612
  7.2 405.1 %all-reduce.6.cloned.1.call-start = ((), (), s32[]{:S(2)}) async-start(), calls=%async_computation.1 | async-start | bytes 1990656 | tf_op jit(solution)/shard_map/psum | solution.py:54
  7.2 95.1 %collective-permute-start = (bf16[24,2,4,160]{3,2,1,0:T(4,128)(2,1)}, bf16[24,2,4,160]{3,2,1,0:T(4,128)(2,1)S(1)}, u32[]{:S(2)}, u32[]{:S(2)}) collective-permute-start(bf16[24,2,4,160]{3,2,1,0:T(4,128)(2,1)} %param.6), channel_id=1, source_target_pairs={{128,0},{256,128},{384,256},{129,1},{257,129},{385,257},{130,2},{2... | collective-permute-start | bytes 184328 | tf_op jit(solution)/shard_map/ppermute | solution.py:12
  102.6 10.1 %collective-permute-start.1 = (bf16[24,4,1,160]{3,2,1,0:T(2,128)(2,1)S(1)}, bf16[24,4,1,160]{3,2,1,0:T(2,128)(2,1)S(1)}, u32[]{:S(2)}, u32[]{:S(2)}) collective-permute-start(bf16[24,4,1,160]{3,2,1,0:T(2,128)(2,1)S(1)} %get-tuple-element.10), channel_id=1, source_target_pairs={{0,16},{16,32},{32,48},{48,64},{64,80},{80,96},{96,112},{1,17},{17... | collective-permute-start | bytes 92168 | tf_op jit(solution)/shard_map/ppermute | solution.py:22
  109.1 5.9 collective-permute-start.2
  130.0 542.5 %all-reduce.4.cloned.1.call-start = ((), (), s32[]{:S(2)}) async-start(), calls=%async_computation | async-start | bytes 3932160 | tf_op jit(solution)/shard_map/psum | solution.py:63
  415.2 260.2 %copy-start = (f32[24,2,4,160]{0,3,2,1:T(8,128)S(1)}, f32[24,2,4,160]{0,3,2,1:T(8,128)}, u32[]{:S(2)}) copy-start(f32[24,2,4,160]{0,3,2,1:T(8,128)} %copy.17) | copy-start | bytes 368644
Sparse Core Ops, SparseCore 0:
  130.1 282.1 all-reduce.5
  415.5 256.9 all-reduce.3
where the time goes:
time: 688 us; the launch traced here: 685 us
  waiting for transfers between devices  533 us (77%)
  blocking collectives  91.9 us (13%)
  local copies, waits for them, and re-layouts  17.4 us (3%)
  between operations  14.3 us (2%)
  other arithmetic  11.7 us (2%)
  starting transfers between devices  9.97 us (1%)
    psum x1, waiting for transfers between devices, on_device(): summed = lax.psum(local_sums, ('tm', 'height'))  274 us
    psum x1, waiting for transfers between devices, on_device(): act_grad = lax.psum(partial_value, 'chan')  257 us
    all_gather x1, blocking collectives, on_device(): whole_x = lax.all_gather(features, 'chan', axis=0, tiled=True)  91.9 us
  transfers between devices with their start and end apart: 5, of which 3 were waited for; matrix products, arithmetic and copies ran while one was open for 2% of the time, Pallas kernels for 0%

commit v1 on v0

v1 whole, which is shorter than its diff:
```python
import functools
import math

import jax
import jax.numpy as jnp
from jax import lax
from jax.experimental import pallas as pl
from jax.experimental.pallas import tpu as pltpu
from jax.sharding import PartitionSpec as P

MESH = pl.DeviceIdType.MESH
SIZES = {"x": 4, "zl": 4, "k": 2, "zh": 4, "y": 4}
CH = 24
TOTAL = 384
LANES = 640
COL = 656
GROWS = 2048
F32 = jnp.float32
BF16 = jnp.bfloat16


def coords():
    t = lax.axis_index("tm")
    h = lax.axis_index("height")
    c = lax.axis_index("chan")
    return {"x": t, "zl": h // 2, "k": h % 2, "zh": c // 4, "y": c % 4}


def shifted(at, **offsets):
    at = dict(at)
    for name, by in offsets.items():
        at[name] = (at[name] + (by % SIZES[name])) % SIZES[name]
    return {"tm": at["x"], "height": at["zl"] * 2 + at["k"], "chan": at["zh"] * 4 + at["y"]}


def neighbour(at, dx, dh):
    t = (at["x"] + (dx % 4)) % 4
    h = (at["zl"] * 2 + at["k"] + (dh % 8)) % 8
    return {"tm": t, "height": h, "chan": at["zh"] * 4 + at["y"]}


HALO = ((-1, 0), (0, 1), (0, -1), (-1, 1), (-1, -1))


def kernel(
    f_ref, d_ref, w_ref, gb_ref, og_ref, od_ref,
    dn, edges, fall, s9, p, pb, ry, q, qb, rz, act, sumsq, inv, dacc, dsend, dmid, dry, drz,
    g, gr, h, hb, hr, zs, zr, ag, ssem, rsem,
):
    at = coords()
    chan = at["zh"] * 4 + at["y"]
    count = [0]

    def send(src, dst, target):
        i = count[0]
        count[0] += 1
        copy = pltpu.make_async_remote_copy(
            src_ref=src, dst_ref=dst, send_sem=ssem.at[i], recv_sem=rsem.at[i],
            device_id=target, device_id_type=MESH,
        )
        copy.start()
        return copy

    barrier = pltpu.get_barrier_semaphore()
    greeted = [neighbour(at, -dx, -dh) for dx, dh in HALO]
    for name in ("x", "zl", "zh", "y"):
        greeted += [shifted(at, **{name: -by}) for by in (1, 2, 3)]
    greeted.append(shifted(at, k=1))
    for one in greeted:
        pl.semaphore_signal(barrier, inc=1, device_id=one, device_id_type=MESH)
    pl.semaphore_wait(barrier, len(greeted))

    started = []
    halo = []
    for n, (dx, dh) in enumerate(HALO):
        if n == 0:
            src, dst = d_ref, dn
        else:
            src = d_ref.at[:, pl.ds(384 if dh == 1 else 0, 256)]
            dst = edges.at[n - 1]
        halo.append(send(src, dst, neighbour(at, dx, dh)))
    fz = {by: send(f_ref, fall.at[chan], shifted(at, zh=by)) for by in (1, 3, 2)}
    fy = []

    def forward(src, block):
        for by in (1, 3, 2):
            fy.append(send(src, fall.at[block], shifted(at, y=by)))

    forward(f_ref, chan)
    fall[chan] = f_ref[...]

    for copy in halo:
        copy.wait_recv()
    lane = lax.broadcasted_iota(jnp.int32, (CH, LANES), 1) % 160
    first, last = lane == 0, lane == 159
    row = at["zl"] * 2 + at["k"]
    top_on = jnp.where(row > 0, 1.0, 0.0).astype(F32)
    bottom_on = jnp.where(row < 7, 1.0, 0.0).astype(F32)
    next_on = jnp.where(at["x"] < 3, 1.0, 0.0).astype(F32)
    for tp in range(4):
        rows = slice(CH * (tp % 2), CH * (tp % 2) + CH)
        late = tp >= 2
        own = (dn if late else d_ref)[...].astype(F32)[rows]
        top = edges[2 if late else 0].astype(F32)[rows] * top_on
        bottom = edges[3 if late else 1].astype(F32)[rows] * bottom_on
        if late:
            own, top, bottom = own * next_on, top * next_on, bottom * next_on
        moved = (
            jnp.concatenate([own[:, 160:], bottom[:, :160]], axis=1),
            own,
            jnp.concatenate([top[:, 96:], own[:, :480]], axis=1),
        )
        pieces = []
        for one in moved:
            pieces.append(jnp.where(last, 0.0, pltpu.roll(one, LANES - 1, 1)))
            pieces.append(one)
            pieces.append(jnp.where(first, 0.0, pltpu.roll(one, 1, 1)))
        s9[tp] = jnp.concatenate(pieces, axis=0).astype(BF16)

    for t in range(2):
        total = None
        for kt in range(3):
            part = jnp.dot(w_ref[kt], s9[t + 2 - kt], preferred_element_type=F32)
            total = part if total is None else total + part
        p[t] = total

    def parts(zh, y):
        start = pl.multiple_of((zh * 4 + y) * CH, 8)
        return jnp.concatenate([p[0, pl.ds(start, CH)], p[1, pl.ds(start, CH)]], axis=0)

    for by in (1, 3):
        fz[by].wait_recv()
        block = (at["zh"] + (4 - by)) % 4 * 4 + at["y"]
        forward(fall.at[block], block)
    ys = []
    for by in (1, 3, 2):
        for zh in range(4):
            pb[by - 1, zh] = parts(zh, (at["y"] + by) % 4).astype(BF16)
        ys.append(send(pb.at[by - 1], ry.at[by - 1], shifted(at, y=by)))
    fz[2].wait_recv()
    block = (at["zh"] + 2) % 4 * 4 + at["y"]
    forward(fall.at[block], block)

    for copy in ys:
        copy.wait_recv()
    zsends = []
    for by in (2, 1, 3, 0):
        zh = (at["zh"] + by) % 4
        value = parts(zh, at["y"])
        for n in range(3):
            value = value + ry[n, zh].astype(F32)
        if by == 0:
            q[...] = value
        else:
            qb[by - 1] = value.astype(BF16)
            zsends.append(send(qb.at[by - 1], rz.at[by - 1], shifted(at, zh=by)))

    for copy in fy:
        copy.wait_recv()
    sumsq[...] = jnp.zeros_like(sumsq)

    @pl.loop(0, 16)
    def _(n):
        value = fall[n].astype(F32)
        sumsq[...] += value * value

    for t in range(2):
        mean = jnp.sum(sumsq[CH * t : CH * t + CH], axis=0, keepdims=True) * (1.0 / TOTAL)
        inv[t : t + 1] = lax.rsqrt(mean + 1e-06)
    dacc[...] = jnp.zeros_like(dacc)

    def activation(x, t, block):
        start = pl.multiple_of(block * CH, 8)
        gain = gb_ref[pl.ds(start, CH), 0:1]
        bias = gb_ref[pl.ds(start, CH), 1:2]
        normed = x * inv[t : t + 1] * gain + bias
        sig = 1.0 / (1.0 + jnp.exp(-normed))
        return normed * sig, sig * (1.0 + normed * (1.0 - sig)) * gain

    @pl.loop(0, 8)
    def _(n):
        even = fall[2 * n].astype(F32)
        odd = fall[2 * n + 1].astype(F32)
        for t in range(2):
            both = []
            for j, block in enumerate((even, odd)):
                x = block[CH * t : CH * t + CH]
                active, slope = activation(x, t, 2 * n + j)
                both.append(active)
                start = pl.multiple_of((2 * n + j) * CH, 8)
                dacc[CH * t : CH * t + CH] += p[t, pl.ds(start, CH)] * slope * x
            act[t, pl.ds(pl.multiple_of(n * 48, 16), 48)] = jnp.concatenate(both, axis=0).astype(BF16)

    for t in range(2):
        dsend[t : t + 1] = jnp.sum(dacc[CH * t : CH * t + CH], axis=0, keepdims=True)
    dys = [send(dsend, dry.at[by - 1], shifted(at, y=by)) for by in (1, 3, 2)]

    for n in range(3):
        g[COL * n + 648 : COL * n + COL] = jnp.zeros((8, 128), F32)
    g[3 * COL : GROWS] = jnp.zeros((GROWS - 3 * COL, 128), F32)
    for kt in range(3):
        total = None
        for t in range(2):
            part = lax.dot_general(
                s9[t + 2 - kt], act[t], (((1,), (1,)), ((), ())), preferred_element_type=F32
            )
            total = part if total is None else total + part
        for n in range(3):
            g[COL * n + 216 * kt : COL * n + 216 * kt + 216] = total[:, 128 * n : 128 * n + 128]
    other = pl.multiple_of((1 - at["k"]) * 1024, 1024)
    mine = pl.multiple_of(at["k"] * 1024, 1024)
    core = send(g.at[pl.ds(other, 1024)], gr, shifted(at, k=1))

    for copy in dys:
        copy.wait_recv()
    dmid[...] = dsend[...] + dry[0] + dry[1] + dry[2]
    dzs = [send(dmid, drz.at[by - 1], shifted(at, zh=by)) for by in (2, 1, 3)]

    core.wait_recv()
    xs = []
    for by in (2, 1, 3, 0):
        start = (at["x"] + by) % 4 * 256
        value = g[pl.ds(pl.multiple_of(mine + start, 256), 256)] + gr[pl.ds(pl.multiple_of(start, 256), 256)]
        if by == 0:
            h[...] = value
        else:
            hb[by - 1] = value.astype(BF16)
            xs.append(send(hb.at[by - 1], hr.at[by - 1], shifted(at, x=by)))
    for copy in xs:
        copy.wait_recv()
    h[...] = h[...] + hr[0].astype(F32) + hr[1].astype(F32) + hr[2].astype(F32)
    zls = []
    for by in (3, 1, 2):
        start = pl.multiple_of((at["zl"] + by) % 4 * 64, 64)
        zs[by - 1] = h[pl.ds(start, 64)]
        zls.append(send(zs.at[by - 1], zr.at[by - 1], shifted(at, zl=by)))
    for copy in zls:
        copy.wait_recv()
    value = h[pl.ds(pl.multiple_of(at["zl"] * 64, 64), 64)] + zr[0] + zr[1] + zr[2]
    base = pl.multiple_of(mine + at["x"] * 256, 256)
    piece = pl.multiple_of(base + at["zl"] * 64, 64)
    ag[pl.ds(piece, 64)] = (value * (1.0 / math.sqrt(40960))).astype(BF16)
    agz = [send(ag.at[pl.ds(piece, 64)], ag.at[pl.ds(piece, 64)], shifted(at, zl=by)) for by in (3, 1, 2)]

    for copy in zsends + dzs:
        copy.wait_recv()
    grad = q[...] + rz[0].astype(F32) + rz[1].astype(F32) + rz[2].astype(F32)
    dots = dmid[...] + drz[0] + drz[1] + drz[2]
    mine_x = f_ref[...].astype(F32)
    ct = d_ref[...].astype(F32)
    outs = []
    for t in range(2):
        rows = slice(CH * t, CH * t + CH)
        x = mine_x[rows]
        _, slope = activation(x, t, chan)
        up = grad[rows] * slope
        r = inv[t : t + 1]
        back = r * up - x * (r * r * r * dots[t : t + 1] * (1.0 / TOTAL))
        outs.append(ct[rows] + back)
    od_ref[...] = jnp.concatenate(outs, axis=0).astype(BF16)

    for copy in agz:
        copy.wait_recv()
    agx = [send(ag.at[pl.ds(base, 256)], ag.at[pl.ds(base, 256)], shifted(at, x=by)) for by in (2, 1, 3)]
    for copy in agx:
        copy.wait_recv()
    last_copy = send(ag.at[pl.ds(mine, 1024)], ag.at[pl.ds(mine, 1024)], shifted(at, k=1))
    last_copy.wait_recv()
    og_ref[...] = ag[...]
    for copy in halo + list(fz.values()) + fy + ys + zsends + dys + [core] + dzs + xs + zls + agz + agx + [last_copy]:
        copy.wait_send()


COPIES = 5 + 3 + 12 + 3 + 3 + 6 + 1 + 3 + 3 + 3 + 3 + 1


def on_device(features, cotangent, conv_weight, norm_gain, norm_bias):
    chans, frames, rows, cols = features.shape
    f = jnp.transpose(features, (1, 0, 2, 3)).reshape(frames * chans, rows * cols)
    d = jnp.transpose(cotangent, (1, 0, 2, 3)).reshape(frames * chans, rows * cols)
    w = jnp.transpose(conv_weight.reshape(chans, 3, 9, TOTAL), (1, 3, 2, 0)).reshape(3, TOTAL, 9 * chans)
    gb = jnp.stack([norm_gain, norm_bias], axis=1)
    vmem = pl.BlockSpec(memory_space=pltpu.VMEM)
    grads, out = pl.pallas_call(
        kernel,
        name="unit_backward",
        out_shape=(
            jax.ShapeDtypeStruct((GROWS, 128), BF16),
            jax.ShapeDtypeStruct((48, LANES), BF16),
        ),
        in_specs=[vmem] * 4,
        out_specs=(vmem, vmem),
        scratch_shapes=[
            pltpu.VMEM((48, LANES), BF16),
            pltpu.VMEM((4, 48, 256), BF16),
            pltpu.VMEM((16, 48, LANES), BF16),
            pltpu.VMEM((4, 216, LANES), BF16),
            pltpu.VMEM((2, TOTAL, LANES), F32),
            pltpu.VMEM((3, 4, 48, LANES), BF16),
            pltpu.VMEM((3, 4, 48, LANES), BF16),
            pltpu.VMEM((48, LANES), F32),
            pltpu.VMEM((3, 48, LANES), BF16),
            pltpu.VMEM((3, 48, LANES), BF16),
            pltpu.VMEM((2, TOTAL, LANES), BF16),
            pltpu.VMEM((48, LANES), F32),
            pltpu.VMEM((2, LANES), F32),
            pltpu.VMEM((48, LANES), F32),
            pltpu.VMEM((2, LANES), F32),
            pltpu.VMEM((2, LANES), F32),
            pltpu.VMEM((3, 2, LANES), F32),
            pltpu.VMEM((3, 2, LANES), F32),
            pltpu.VMEM((GROWS, 128), F32),
            pltpu.VMEM((1024, 128), F32),
            pltpu.VMEM((256, 128), F32),
            pltpu.VMEM((3, 256, 128), BF16),
            pltpu.VMEM((3, 256, 128), BF16),
            pltpu.VMEM((3, 64, 128), F32),
            pltpu.VMEM((3, 64, 128), F32),
            pltpu.VMEM((GROWS, 128), BF16),
            pltpu.SemaphoreType.DMA((COPIES,)),
            pltpu.SemaphoreType.DMA((COPIES,)),
        ],
        compiler_params=pltpu.CompilerParams(
            collective_id=0, has_side_effects=True, vmem_limit_bytes=40 << 20
        ),
    )(f, d, w, gb)
    result = jnp.transpose(out.reshape(frames, chans, rows, cols), (1, 0, 2, 3))
    flat = jnp.concatenate([grads[COL * n : COL * n + 648] for n in range(3)], axis=1)
    weight_grad = jnp.transpose(flat.reshape(27, chans, TOTAL), (1, 0, 2)).astype(F32)
    return result, weight_grad


def solution(mesh):
    return jax.shard_map(
        on_device,
        mesh=mesh,
        in_specs=(
            P("chan", "tm", "height", None),
            P("chan", "tm", "height", None),
            P("chan", None, None),
            P(),
            P(),
        ),
        out_specs=(P("chan", "tm", "height", None), P("chan", None, None)),
        check_vma=False,
    )
```

time: 688 us -> 80 us (0.12)
  waiting for transfers between devices: 533 us -> 0 us
  blocking collectives: 91.9 us -> 0 us
  Pallas kernels: 0 us -> 73.2 us
  between operations: 14.3 us -> 0.73 us
  local copies, waits for them, and re-layouts: 17.4 us -> 4.73 us
  other arithmetic: 11.7 us -> 1.09 us
  starting transfers between devices: 9.97 us -> 0 us
    psum x2 -> x0, waiting for transfers between devices: 531 us -> none  [the longest x1 274 us: on_device(): summed = lax.psum(local_sums, ('tm', 'height'))]
    all_gather x1 -> x0, blocking collectives: 91.9 us -> none  [on_device(): whole_x = lax.all_gather(features, 'chan', axis=0, tiled=True)]
    pallas_call x0 -> x1, Pallas kernels: none -> 73.2 us  [on_device(): pl.pallas_call(kernel, name='unit_backward', out_shape=(jax.ShapeDtypeStr...]
    ppermute x3 -> x0, starting transfers between devices: 9.71 us -> none  [the longest x1 6.49 us: with_halo(): before = lax.ppermute(last, axis, up)]
  transfers between devices with their start and end apart: 5 -> 0, of which waited for: 3 -> 0; matrix products, arithmetic and copies ran while one was open for 2% -> 0% of each run, Pallas kernels for 0% -> 0%
where the time goes in v1:
time: 80 us; the launch traced here: 79.7 us
  Pallas kernels  73.2 us (92%)
  local copies, waits for them, and re-layouts  4.73 us (6%)
  other arithmetic  1.09 us (1%)
    pallas_call x1, Pallas kernels, on_device(): pl.pallas_call(kernel, name='unit_backward', out_shape=(jax.ShapeDtypeStr...  73.2 us
    unnamed x8, local copies, waits for them, and re-layouts  2.18 us

profile of v1, /device:TPU:1, one launch (start us, length us, event | category | flops | bytes accessed | tf_op | source)
XLA Modules:
  0.0 79.7 jit_solution(6824030099745401160)
XLA Ops:
  0.6 0.0 copy-start.2
  0.6 1.3 %copy.19.w_ref = bf16[3,384,216]{2,1,0:T(8,128)(2,1)S(1)} copy(bf16[3,384,216]{1,2,0:T(8,128)(2,1)} %bitcast.15) | data formatting | bytes 995328 | tf_op jit(solution)/shard_map/reshape | solution.py:281
  1.9 0.0 copy-done.2
  1.9 0.0 copy-start.3
  2.0 0.7 copy-done.3
  2.6 0.0 copy-start
  2.6 0.1 copy.20.gb_ref
  2.8 0.7 copy-done
  3.6 0.0 copy-start.1
  3.6 0.1 reshape.22.f_ref
  3.7 0.8 copy-done.1
  4.5 0.1 reshape.23.d_ref
  4.6 73.2 %unit_backward.1 = (bf16[2048,128]{1,0:T(8,128)(2,1)S(1)}, bf16[48,640]{1,0:T(8,128)(2,1)S(1)}) custom-call(bf16[48,640]{1,0:T(8,128)(2,1)S(1)} %reshape.22.f_ref, bf16[48,640]{1,0:T(8,128)(2,1)S(1)} %reshape.23.d_ref, bf16[3,384,216]{2,1,0:T(8,128)(2,1)S(1)} %copy.19.w_ref, f32[384,2]{1,0:T(8,128)S(1)} %copy.20.gb_ref), custom_call_target="tpu_custom_call" | custom-call | tf_op jit(solution)/shard_map/unit_backward/pallas_call | solution.py:284
  77.8 0.1 pad_maximum_fusion
  77.9 1.0 %convert_bitcast_fusion = f32[24,27,384]{2,0,1:T(8,128)} fusion(bf16[27,24,384]{2,1,0:T(8,128)(2,1)S(1)} %bitcast.14), kind=kLoop, calls=%fused_computation | loop fusion | flops 248832 | bytes 1492992 | tf_op jit(solution)/shard_map/convert_element_type | solution.py:329
  78.9 0.1 reshape.26
  79.1 0.7 copy.23
  (6 shorter events, 0.1 us)
Async XLA Ops:
  0.6 1.3 %copy-start.2 = (f32[384]{0:T(512)S(1)}, f32[384]{0:T(512)}, u32[]{:S(2)}) copy-start(f32[384]{0:T(512)} %param.9) | copy-start | bytes 4612
  1.9 0.7 copy-start.3
  2.6 0.9 %copy-start = (bf16[24,2,4,160]{3,2,1,0:T(4,128)(2,1)S(1)}, bf16[24,2,4,160]{3,2,1,0:T(4,128)(2,1)}, u32[]{:S(2)}) copy-start(bf16[24,2,4,160]{3,2,1,0:T(4,128)(2,1)} %param.5) | copy-start | bytes 184324
  3.6 0.9 %copy-start.1 = (bf16[24,2,4,160]{3,2,1,0:T(4,128)(2,1)S(1)}, bf16[24,2,4,160]{3,2,1,0:T(4,128)(2,1)}, u32[]{:S(2)}) copy-start(bf16[24,2,4,160]{3,2,1,0:T(4,128)(2,1)} %param.6) | copy-start | bytes 184324

commit v2 on v1

v2 whole, which is shorter than its diff:
```python
import functools
import math

import jax
import jax.numpy as jnp
from jax import lax
from jax.experimental import pallas as pl
from jax.experimental.pallas import tpu as pltpu
from jax.sharding import PartitionSpec as P

MESH = pl.DeviceIdType.MESH
SIZES = {"x": 4, "zl": 4, "k": 2, "zh": 4, "y": 4}
CH = 24
TOTAL = 384
LANES = 640
F32 = jnp.float32
BF16 = jnp.bfloat16


def coords():
    t = lax.axis_index("tm")
    h = lax.axis_index("height")
    c = lax.axis_index("chan")
    return {"x": t, "zl": h // 2, "k": h % 2, "zh": c // 4, "y": c % 4}


def shifted(at, **offsets):
    at = dict(at)
    for name, by in offsets.items():
        at[name] = (at[name] + (by % SIZES[name])) % SIZES[name]
    return {"tm": at["x"], "height": at["zl"] * 2 + at["k"], "chan": at["zh"] * 4 + at["y"]}


def neighbour(at, dx, dh):
    t = (at["x"] + (dx % 4)) % 4
    h = (at["zl"] * 2 + at["k"] + (dh % 8)) % 8
    return {"tm": t, "height": h, "chan": at["zh"] * 4 + at["y"]}


HALO = ((-1, 0), (0, 1), (0, -1), (-1, 1), (-1, -1))
FIRST, FAR = 3 * 512, 512
COPIES = 80


def kernel(
    f_ref, d_ref, w_ref, gb_ref, og_ref, od_ref,
    dn, edges, fall, s9, p, pb, ry, q, qb, rz, actx, acty, inv, dacc,
    sown, smid, sry, srz, dsend, dmid, dry, drz, gc, first_bufs, far_bufs, ssem, rsem,
):
    at = coords()
    chan = at["zh"] * 4 + at["y"]
    count = [0]
    started = []

    def send(src, dst, target):
        i = count[0]
        count[0] += 1
        copy = pltpu.make_async_remote_copy(
            src_ref=src, dst_ref=dst, send_sem=ssem.at[i], recv_sem=rsem.at[i],
            device_id=target, device_id_type=MESH,
        )
        copy.start()
        started.append(copy)
        return copy

    def arrived(copies):
        for copy in copies:
            copy.wait_recv()

    barrier = pltpu.get_barrier_semaphore()
    greeted = [shifted(at, zh=1), shifted(at, zh=3)]
    greeted += [neighbour(at, -dx, -dh) for dx, dh in HALO]
    for name in ("y", "x", "zl"):
        greeted += [shifted(at, **{name: by}) for by in (1, 2, 3)]
    greeted.append(shifted(at, k=1))
    for one in greeted:
        pl.semaphore_signal(barrier, inc=1, device_id=one, device_id_type=MESH)

    fall[chan] = f_ref[...]
    squares = f_ref[...].astype(F32)
    squares = squares * squares
    for t in range(2):
        sown[t : t + 1] = jnp.sum(squares[CH * t : CH * t + CH], axis=0, keepdims=True)
    pl.semaphore_wait(barrier, len(greeted))

    fz = [send(f_ref, fall.at[chan], shifted(at, zh=by)) for by in (1, 3)]
    halo = []
    for n, (dx, dh) in enumerate(HALO):
        if n == 0:
            src, dst = d_ref, dn
        else:
            src = d_ref.at[:, pl.ds(384 if dh == 1 else 0, 256)]
            dst = edges.at[n - 1]
        halo.append(send(src, dst, neighbour(at, dx, dh)))
    sys = [send(sown, sry.at[by - 1], shifted(at, y=by)) for by in (2, 1, 3)]

    def forward(src, block):
        return [send(src, fall.at[block], shifted(at, y=by)) for by in (2, 1, 3)]

    fy_own = forward(f_ref, chan)

    arrived(halo)
    lane = lax.broadcasted_iota(jnp.int32, (CH, LANES), 1) % 160
    left_end, right_end = lane == 0, lane == 159
    row = at["zl"] * 2 + at["k"]
    top_on = jnp.where(row > 0, 1.0, 0.0).astype(F32)
    bottom_on = jnp.where(row < 7, 1.0, 0.0).astype(F32)
    next_on = jnp.where(at["x"] < 3, 1.0, 0.0).astype(F32)
    for tp in range(4):
        rows = slice(CH * (tp % 2), CH * (tp % 2) + CH)
        late = tp >= 2
        own = (dn if late else d_ref)[...].astype(F32)[rows]
        top = edges[2 if late else 0].astype(F32)[rows] * top_on
        bottom = edges[3 if late else 1].astype(F32)[rows] * bottom_on
        if late:
            own, top, bottom = own * next_on, top * next_on, bottom * next_on
        moved = (
            jnp.concatenate([own[:, 160:], bottom[:, :160]], axis=1),
            own,
            jnp.concatenate([top[:, 96:], own[:, :480]], axis=1),
        )
        pieces = []
        for one in moved:
            pieces.append(jnp.where(right_end, 0.0, pltpu.roll(one, LANES - 1, 1)))
            pieces.append(one)
            pieces.append(jnp.where(left_end, 0.0, pltpu.roll(one, 1, 1)))
        s9[tp] = jnp.concatenate(pieces, axis=0).astype(BF16)

    arrived(sys)
    smid[0] = sown[...] + sry[0] + sry[1] + sry[2]
    szs = [send(smid.at[0], smid.at[by], shifted(at, zh=by)) for by in (1, 3)]

    for t in range(2):
        total = None
        for kt in range(3):
            part = jnp.dot(w_ref[kt], s9[t + 2 - kt], preferred_element_type=F32)
            total = part if total is None else total + part
        p[t] = total

    def parts(zh, y):
        start = pl.multiple_of((zh * 4 + y) * CH, 8)
        return jnp.concatenate([p[0, pl.ds(start, CH)], p[1, pl.ds(start, CH)]], axis=0)

    ys = []
    for by in (2, 1, 3):
        for zh in range(4):
            pb[by - 1, zh] = parts(zh, (at["y"] + by) % 4).astype(BF16)
        ys.append(send(pb.at[by - 1], ry.at[by - 1], shifted(at, y=by)))

    def block_at(by):
        return (at["zh"] + by) % 4 * 4 + at["y"]

    side = 1 + 2 * at["k"]
    arrived(fz)
    source = (at["zh"] + side) % 4 * 4 + at["y"]
    away = {"tm": at["x"], "height": row, "chan": (at["zh"] + 4 - side) % 4 * 4 + at["y"]}
    fz_far = send(fall.at[source], fall.at[source], away)
    fy_near = forward(fall.at[block_at(3)], block_at(3)) + forward(fall.at[block_at(1)], block_at(1))

    arrived(szs)
    szf = send(smid.at[1], srz, shifted(at, zh=1))
    arrived([szf])
    total = smid[0] + smid[1] + smid[3] + srz[...]
    inv[...] = lax.rsqrt(total * (1.0 / TOTAL) + 1e-06)
    dacc[...] = jnp.zeros_like(dacc)

    def activation(x, t, block):
        start = pl.multiple_of(block * CH, 8)
        gain = gb_ref[pl.ds(start, CH), 0:1]
        bias = gb_ref[pl.ds(start, CH), 1:2]
        normed = x * inv[t : t + 1] * gain + bias
        sig = 1.0 / (1.0 + jnp.exp(-normed))
        return normed * sig, sig * (1.0 + normed * (1.0 - sig)) * gain

    def activate(by, dst, base):
        zh = (at["zh"] + by) % 4

        @pl.loop(0, 2)
        def _(n):
            blocks = [fall[zh * 4 + 2 * n + j].astype(F32) for j in range(2)]
            for t in range(2):
                both = []
                for j in range(2):
                    x = blocks[j][CH * t : CH * t + CH]
                    active, slope = activation(x, t, zh * 4 + 2 * n + j)
                    both.append(active)
                    start = pl.multiple_of((zh * 4 + 2 * n + j) * CH, 8)
                    dacc[CH * t : CH * t + CH] += p[t, pl.ds(start, CH)] * slope * x
                dst[t, pl.ds(pl.multiple_of(base + n * 48, 16), 48)] = jnp.concatenate(both, axis=0).astype(BF16)

    def weigh(act, base, g, at_row):
        for kt in range(3):
            total = None
            for t in range(2):
                part = lax.dot_general(
                    s9[t + 2 - kt], act[t, base : base + 96], (((1,), (1,)), ((), ())), preferred_element_type=F32
                )
                total = part if total is None else total + part
            gc[216 * kt : 216 * kt + 216] = total
        g[at_row : at_row + 328] = jnp.concatenate([gc[0:328, 0:64], gc[320:648, 0:64]], axis=1)
        g[at_row + 328 : at_row + 496] = jnp.concatenate(
            [gc[160 * n : 160 * n + 168, 64:96] for n in range(4)], axis=1
        )

    first_g, far_g = first_bufs[0], far_bufs[0]
    first_g[1488:FIRST] = jnp.zeros((FIRST - 1488, 128), F32)
    far_g[496:FAR] = jnp.zeros((FAR - 496, 128), F32)

    arrived(fy_own)
    activate(0, actx, 0)
    weigh(actx, 0, first_g, 0)
    arrived([fz_far])
    fy_far = forward(fall.at[block_at(2)], block_at(2))

    arrived(ys)
    zsends = []
    for by in (2, 1, 3, 0):
        zh = (at["zh"] + by) % 4
        value = parts(zh, at["y"])
        for n in range(3):
            value = value + ry[n, zh].astype(F32)
        if by == 0:
            q[...] = value
        else:
            qb[by - 1] = value.astype(BF16)
            zsends.append(send(qb.at[by - 1], rz.at[by - 1], shifted(at, zh=by)))

    def core_reduce(bufs, size):
        g, gr = bufs[0], bufs[1]
        other = pl.multiple_of((1 - at["k"]) * (size // 2), size // 2)
        return send(g.at[pl.ds(other, size // 2)], gr, shifted(at, k=1))

    def x_reduce(bufs, size):
        g, gr, h, hb, hr = bufs[:5]
        quarter = size // 8
        sends = []
        for by in (2, 1, 3, 0):
            start = (at["x"] + by) % 4 * quarter
            value = (
                g[pl.ds(pl.multiple_of(at["k"] * (size // 2) + start, quarter), quarter)]
                + gr[pl.ds(pl.multiple_of(start, quarter), quarter)]
            )
            if by == 0:
                h[...] = value
            else:
                hb[by - 1] = value.astype(BF16)
                sends.append(send(hb.at[by - 1], hr.at[by - 1], shifted(at, x=by)))
        return sends

    def z_reduce(bufs, size):
        h, hr, zs, zr = bufs[2], bufs[4], bufs[5], bufs[6]
        part = size // 32
        h[...] = h[...] + hr[0].astype(F32) + hr[1].astype(F32) + hr[2].astype(F32)
        sends = []
        for by in (3, 1, 2):
            start = pl.multiple_of((at["zl"] + by) % 4 * part, part)
            zs[by - 1] = h[pl.ds(start, part)]
            sends.append(send(zs.at[by - 1], zr.at[by - 1], shifted(at, zl=by)))
        return sends

    def z_gather(bufs, size):
        h, zr, ag = bufs[2], bufs[6], bufs[7]
        part = size // 32
        value = h[pl.ds(pl.multiple_of(at["zl"] * part, part), part)] + zr[0] + zr[1] + zr[2]
        piece = pl.multiple_of(at["k"] * (size // 2) + at["x"] * (size // 8) + at["zl"] * part, part)
        ag[pl.ds(piece, part)] = (value * (1.0 / math.sqrt(40960))).astype(BF16)
        ref = ag.at[pl.ds(piece, part)]
        return [send(ref, ref, shifted(at, zl=by)) for by in (3, 1, 2)]

    def x_gather(bufs, size):
        start = pl.multiple_of(at["k"] * (size // 2) + at["x"] * (size // 8), size // 8)
        ref = bufs[7].at[pl.ds(start, size // 8)]
        return [send(ref, ref, shifted(at, x=by)) for by in (2, 1, 3)]

    def core_gather(bufs, size):
        ref = bufs[7].at[pl.ds(pl.multiple_of(at["k"] * (size // 2), size // 2), size // 2)]
        return send(ref, ref, shifted(at, k=1))

    def deliver(bufs, n, by):
        value = bufs[7][496 * n : 496 * n + 496].astype(F32)
        low, high = value[:328], value[328:]
        left = jnp.concatenate([low[:, :64], low[8:, 64:]], axis=0)
        right = jnp.concatenate(
            [high[:, :32], high[8:, 32:64], high[8:, 64:96], high[8:, 96:]], axis=0
        )
        og_ref[(at["zh"] + by) % 4] = jnp.concatenate([left, right], axis=1).astype(BF16)

    arrived(fy_near)
    activate(1, actx, 96)
    activate(3, actx, 192)
    weigh(actx, 96, first_g, 496)
    weigh(actx, 192, first_g, 992)
    a = core_reduce(first_bufs, FIRST)
    arrived(fy_far)
    activate(2, acty, 0)
    for t in range(2):
        dsend[t : t + 1] = jnp.sum(dacc[CH * t : CH * t + CH], axis=0, keepdims=True)
    dys = [send(dsend, dry.at[by - 1], shifted(at, y=by)) for by in (2, 1, 3)]
    arrived([a])
    a = x_reduce(first_bufs, FIRST)
    weigh(acty, 0, far_g, 0)
    b = core_reduce(far_bufs, FAR)
    arrived(dys)
    dmid[...] = dsend[...] + dry[0] + dry[1] + dry[2]
    dzs = [send(dmid, drz.at[by - 1], shifted(at, zh=by)) for by in (2, 1, 3)]
    arrived([b])
    b = x_reduce(far_bufs, FAR)
    arrived(a)
    a = z_reduce(first_bufs, FIRST)
    arrived(b)
    b = z_reduce(far_bufs, FAR)
    arrived(a)
    a = z_gather(first_bufs, FIRST)
    arrived(b)
    b = z_gather(far_bufs, FAR)
    arrived(a)
    a = x_gather(first_bufs, FIRST)
    arrived(b)
    b = x_gather(far_bufs, FAR)

    arrived(zsends + dzs)
    grad = q[...] + rz[0].astype(F32) + rz[1].astype(F32) + rz[2].astype(F32)
    dots = dmid[...] + drz[0] + drz[1] + drz[2]
    mine_x = f_ref[...].astype(F32)
    ct = d_ref[...].astype(F32)
    outs = []
    for t in range(2):
        rows = slice(CH * t, CH * t + CH)
        x = mine_x[rows]
        _, slope = activation(x, t, chan)
        up = grad[rows] * slope
        r = inv[t : t + 1]
        back = r * up - x * (r * r * r * dots[t : t + 1] * (1.0 / TOTAL))
        outs.append(ct[rows] + back)
    od_ref[...] = jnp.concatenate(outs, axis=0).astype(BF16)

    arrived(a)
    a = core_gather(first_bufs, FIRST)
    arrived(b)
    b = core_gather(far_bufs, FAR)
    arrived([a])
    deliver(first_bufs, 0, 0)
    deliver(first_bufs, 1, 1)
    deliver(first_bufs, 2, 3)
    arrived([b])
    deliver(far_bufs, 0, 2)
    for copy in started:
        copy.wait_send()


def chain_buffers(size):
    return [
        pltpu.VMEM((size, 128), F32),
        pltpu.VMEM((size // 2, 128), F32),
        pltpu.VMEM((size // 8, 128), F32),
        pltpu.VMEM((3, size // 8, 128), BF16),
        pltpu.VMEM((3, size // 8, 128), BF16),
        pltpu.VMEM((3, size // 32, 128), F32),
        pltpu.VMEM((3, size // 32, 128), F32),
        pltpu.VMEM((size, 128), BF16),
    ]


def on_device(features, cotangent, conv_weight, norm_gain, norm_bias):
    chans, frames, rows, cols = features.shape
    f = jnp.transpose(features, (1, 0, 2, 3)).reshape(frames * chans, rows * cols)
    d = jnp.transpose(cotangent, (1, 0, 2, 3)).reshape(frames * chans, rows * cols)
    w = jnp.transpose(conv_weight.reshape(chans, 3, 9, TOTAL), (1, 3, 2, 0)).reshape(3, TOTAL, 9 * chans)
    gb = jnp.stack([norm_gain, norm_bias], axis=1)
    vmem = pl.BlockSpec(memory_space=pltpu.VMEM)
    sums = pltpu.VMEM((2, LANES), F32)
    grads, out = pl.pallas_call(
        kernel,
        name="unit_backward",
        out_shape=(
            jax.ShapeDtypeStruct((4, 648, 96), BF16),
            jax.ShapeDtypeStruct((48, LANES), BF16),
        ),
        in_specs=[vmem] * 4,
        out_specs=(vmem, vmem),
        scratch_shapes=[
            pltpu.VMEM((48, LANES), BF16),
            pltpu.VMEM((4, 48, 256), BF16),
            pltpu.VMEM((16, 48, LANES), BF16),
            pltpu.VMEM((4, 216, LANES), BF16),
            pltpu.VMEM((2, TOTAL, LANES), F32),
            pltpu.VMEM((3, 4, 48, LANES), BF16),
            pltpu.VMEM((3, 4, 48, LANES), BF16),
            pltpu.VMEM((48, LANES), F32),
            pltpu.VMEM((3, 48, LANES), BF16),
            pltpu.VMEM((3, 48, LANES), BF16),
            pltpu.VMEM((2, 288, LANES), BF16),
            pltpu.VMEM((2, 96, LANES), BF16),
            sums,
            pltpu.VMEM((48, LANES), F32),
            sums,
            pltpu.VMEM((4, 2, LANES), F32),
            pltpu.VMEM((3, 2, LANES), F32),
            sums,
            sums,
            sums,
            pltpu.VMEM((3, 2, LANES), F32),
            pltpu.VMEM((3, 2, LANES), F32),
            pltpu.VMEM((648, 96), F32),
            chain_buffers(FIRST),
            chain_buffers(FAR),
            pltpu.SemaphoreType.DMA((COPIES,)),
            pltpu.SemaphoreType.DMA((COPIES,)),
        ],
        compiler_params=pltpu.CompilerParams(
            collective_id=0, has_side_effects=True, vmem_limit_bytes=40 << 20
        ),
    )(f, d, w, gb)
    result = jnp.transpose(out.reshape(frames, chans, rows, cols), (1, 0, 2, 3))
    flat = jnp.transpose(grads, (1, 0, 2)).reshape(27, chans, TOTAL)
    weight_grad = jnp.transpose(flat, (1, 0, 2)).astype(F32)
    return result, weight_grad


def solution(mesh):
    return jax.shard_map(
        on_device,
        mesh=mesh,
        in_specs=(
            P("chan", "tm", "height", None),
            P("chan", "tm", "height", None),
            P("chan", None, None),
            P(),
            P(),
        ),
        out_specs=(P("chan", "tm", "height", None), P("chan", None, None)),
        check_vma=False,
    )
```

time: 80 us -> 73.5 us (0.919)
  Pallas kernels: 73.2 us -> 66.6 us
  local copies, waits for them, and re-layouts: 4.73 us -> 5.85 us
  other arithmetic: 1.09 us -> 0.1 us
    pallas_call x1, Pallas kernels: 73.2 us -> 66.6 us  [on_device(): pl.pallas_call(kernel, name='unit_backward', out_shape=(jax.ShapeDtypeStr...]
    unnamed x8 -> x4, local copies, waits for them, and re-layouts: 2.18 us -> 0.01 us
    convert_element_type x0 -> x2, local copies, waits for them, and re-layouts: none -> 1.93 us  [on_device(): weight_grad = jnp.transpose(flat, (1, 0, 2)).astype(F32)]
    another operation x3, local copies, waits for them, and re-layouts: 0.14 us -> 1.51 us  [on_device(): gb = jnp.stack([norm_gain, norm_bias], axis=1)]
    convert_element_type x1, other arithmetic: 1.01 us -> 0.09 us  [on_device(): weight_grad = jnp.transpose(flat, (1, 0, 2)).astype(F32)]
where the time goes in v2:
time: 73.5 us; the launch traced here: 73.3 us
  Pallas kernels  66.6 us (91%)
  local copies, waits for them, and re-layouts  5.85 us (8%)
    pallas_call x1, Pallas kernels, on_device(): pl.pallas_call(kernel, name='unit_backward', out_shape=(jax.ShapeDtypeStr...  66.6 us
    convert_element_type x2, local copies, waits for them, and re-layouts, on_device(): weight_grad = jnp.transpose(flat, (1, 0, 2)).astype(F32)  1.93 us
    another operation x3, local copies, waits for them, and re-layouts, on_device(): gb = jnp.stack([norm_gain, norm_bias], axis=1)  1.51 us

profile of v2, /device:TPU:1, one launch (start us, length us, event | category | flops | bytes accessed | tf_op | source)
XLA Modules:
  0.0 73.3 jit_solution(394009966734320949)
XLA Ops:
  0.6 0.0 copy-start
  0.6 0.0 copy-start.1
  0.6 1.3 %copy.20.w_ref = bf16[3,384,216]{2,1,0:T(8,128)(2,1)S(1)} copy(bf16[3,384,216]{1,2,0:T(8,128)(2,1)} %bitcast.14) | data formatting | bytes 995328 | tf_op jit(solution)/shard_map/reshape | solution.py:368
  2.0 0.7 stack.10
  2.6 0.7 stack.9
  3.3 0.1 copy.21.gb_ref
  3.5 0.0 copy-done
  3.5 0.1 reshape.22.f_ref
  3.7 0.0 copy-done.1
  3.7 0.1 reshape.23.d_ref
  3.8 66.6 %unit_backward.1 = (bf16[4,648,96]{2,1,0:T(8,128)(2,1)S(1)}, bf16[48,640]{1,0:T(8,128)(2,1)S(1)}) custom-call(bf16[48,640]{1,0:T(8,128)(2,1)S(1)} %reshape.22.f_ref, bf16[48,640]{1,0:T(8,128)(2,1)S(1)} %reshape.23.d_ref, bf16[3,384,216]{2,1,0:T(8,128)(2,1)S(1)} %copy.20.w_ref, f32[384,2]{1,0:T(8,128)S(1)} %copy.21.gb_ref), custom_call_target="tpu_custom_call" | custom-call | tf_op jit(solution)/shard_map/unit_backward/pallas_call | solution.py:372
  70.5 0.1 convert_bitcast_fusion
  70.6 0.3 copy.23
  70.9 1.6 %reshape.27 = f32[27,24,384]{2,1,0:T(8,128)} reshape(f32[648,4,96]{2,1,0:T(4,128)S(1)} %copy.23) | data formatting | bytes 1990656 | tf_op jit(solution)/shard_map/convert_element_type | solution.py:416
  72.5 0.1 reshape.26
  72.6 0.7 copy.25
  (3 shorter events, 0.1 us)
Async XLA Ops:
  0.6 2.9 %copy-start = (bf16[24,2,4,160]{3,2,1,0:T(4,128)(2,1)S(1)}, bf16[24,2,4,160]{3,2,1,0:T(4,128)(2,1)}, u32[]{:S(2)}) copy-start(bf16[24,2,4,160]{3,2,1,0:T(4,128)(2,1)} %param.5) | copy-start | bytes 184324
  0.6 3.0 %copy-start.1 = (bf16[24,2,4,160]{3,2,1,0:T(4,128)(2,1)S(1)}, bf16[24,2,4,160]{3,2,1,0:T(4,128)(2,1)}, u32[]{:S(2)}) copy-start(bf16[24,2,4,160]{3,2,1,0:T(4,128)(2,1)} %param.6) | copy-start | bytes 184324

commit v3 on v2

--- a/solution.py
+++ b/solution.py
@@ -39,7 +39,7 @@
 
 HALO = ((-1, 0), (0, 1), (0, -1), (-1, 1), (-1, -1))
 FIRST, FAR = 3 * 512, 512
-COPIES = 80
+COPIES = 96
 
 
 def kernel(
@@ -83,7 +83,6 @@
         sown[t : t + 1] = jnp.sum(squares[CH * t : CH * t + CH], axis=0, keepdims=True)
     pl.semaphore_wait(barrier, len(greeted))
 
-    fz = [send(f_ref, fall.at[chan], shifted(at, zh=by)) for by in (1, 3)]
     halo = []
     for n, (dx, dh) in enumerate(HALO):
         if n == 0:
@@ -92,6 +91,7 @@
             src = d_ref.at[:, pl.ds(384 if dh == 1 else 0, 256)]
             dst = edges.at[n - 1]
         halo.append(send(src, dst, neighbour(at, dx, dh)))
+    fz = [send(f_ref, fall.at[chan], shifted(at, zh=by)) for by in (1, 3)]
     sys = [send(sown, sry.at[by - 1], shifted(at, y=by)) for by in (2, 1, 3)]
 
     def forward(src, block):
@@ -141,11 +141,14 @@
         start = pl.multiple_of((zh * 4 + y) * CH, 8)
         return jnp.concatenate([p[0, pl.ds(start, CH)], p[1, pl.ds(start, CH)]], axis=0)
 
-    ys = []
-    for by in (2, 1, 3):
-        for zh in range(4):
-            pb[by - 1, zh] = parts(zh, (at["y"] + by) % 4).astype(BF16)
-        ys.append(send(pb.at[by - 1], ry.at[by - 1], shifted(at, y=by)))
+    ys = {}
+
+    def reduce_y(z_by):
+        for by in (2, 1, 3):
+            pb[by - 1, z_by] = parts((at["zh"] + z_by) % 4, (at["y"] + by) % 4).astype(BF16)
+        ys[z_by] = [send(pb.at[by - 1, z_by], ry.at[by - 1, z_by], shifted(at, y=by)) for by in (2, 1, 3)]
+
+    reduce_y(2)
 
     def block_at(by):
         return (at["zh"] + by) % 4 * 4 + at["y"]
@@ -156,6 +159,9 @@
     away = {"tm": at["x"], "height": row, "chan": (at["zh"] + 4 - side) % 4 * 4 + at["y"]}
     fz_far = send(fall.at[source], fall.at[source], away)
     fy_near = forward(fall.at[block_at(3)], block_at(3)) + forward(fall.at[block_at(1)], block_at(1))
+    reduce_y(1)
+    reduce_y(3)
+    reduce_y(0)
 
     arrived(szs)
     szf = send(smid.at[1], srz, shifted(at, zh=1))
@@ -206,24 +212,25 @@
     first_g[1488:FIRST] = jnp.zeros((FIRST - 1488, 128), F32)
     far_g[496:FAR] = jnp.zeros((FAR - 496, 128), F32)
 
-    arrived(fy_own)
-    activate(0, actx, 0)
-    weigh(actx, 0, first_g, 0)
-    arrived([fz_far])
-    fy_far = forward(fall.at[block_at(2)], block_at(2))
-
-    arrived(ys)
     zsends = []
-    for by in (2, 1, 3, 0):
-        zh = (at["zh"] + by) % 4
-        value = parts(zh, at["y"])
+
+    def reduce_z(by):
+        arrived(ys[by])
+        value = parts((at["zh"] + by) % 4, at["y"])
         for n in range(3):
-            value = value + ry[n, zh].astype(F32)
+            value = value + ry[n, by].astype(F32)
         if by == 0:
             q[...] = value
         else:
             qb[by - 1] = value.astype(BF16)
             zsends.append(send(qb.at[by - 1], rz.at[by - 1], shifted(at, zh=by)))
+
+    arrived(fy_own)
+    activate(0, actx, 0)
+    weigh(actx, 0, first_g, 0)
+    reduce_z(2)
+    arrived([fz_far])
+    fy_far = forward(fall.at[block_at(2)], block_at(2))
 
     def core_reduce(bufs, size):
         g, gr = bufs[0], bufs[1]
@@ -287,9 +294,11 @@
 
     arrived(fy_near)
     activate(1, actx, 96)
+    weigh(actx, 96, first_g, 496)
+    reduce_z(1)
     activate(3, actx, 192)
-    weigh(actx, 96, first_g, 496)
     weigh(actx, 192, first_g, 992)
+    reduce_z(3)
     a = core_reduce(first_bufs, FIRST)
     arrived(fy_far)
     activate(2, acty, 0)
@@ -302,6 +311,7 @@
     b = core_reduce(far_bufs, FAR)
     arrived(dys)
     dmid[...] = dsend[...] + dry[0] + dry[1] + dry[2]
+    reduce_z(0)
     dzs = [send(dmid, drz.at[by - 1], shifted(at, zh=by)) for by in (2, 1, 3)]
     arrived([b])
     b = x_reduce(far_bufs, FAR)

time: 73.5 us -> 70.2 us (0.955)
  Pallas kernels: 66.6 us -> 63.3 us
    pallas_call x1, Pallas kernels: 66.6 us -> 63.3 us  [on_device(): pl.pallas_call(kernel, name='unit_backward', out_shape=(jax.ShapeDtypeStr...]
where the time goes in v3:
time: 70.2 us; the launch traced here: 70 us
  Pallas kernels  63.3 us (90%)
  local copies, waits for them, and re-layouts  5.85 us (8%)
  between operations  0.73 us (1%)
    pallas_call x1, Pallas kernels, on_device(): pl.pallas_call(kernel, name='unit_backward', out_shape=(jax.ShapeDtypeStr...  63.3 us
    convert_element_type x2, local copies, waits for them, and re-layouts, on_device(): weight_grad = jnp.transpose(flat, (1, 0, 2)).astype(F32)  1.93 us
    another operation x3, local copies, waits for them, and re-layouts, on_device(): gb = jnp.stack([norm_gain, norm_bias], axis=1)  1.51 us

profile of v3, /device:TPU:1, one launch (start us, length us, event | category | flops | bytes accessed | tf_op | source)
XLA Modules:
  0.0 70.0 jit_solution(11651256125498427021)
XLA Ops:
  0.6 0.0 copy-start
  0.6 0.0 copy-start.1
  0.6 1.3 %copy.20.w_ref = bf16[3,384,216]{2,1,0:T(8,128)(2,1)S(1)} copy(bf16[3,384,216]{1,2,0:T(8,128)(2,1)} %bitcast.14) | data formatting | bytes 995328 | tf_op jit(solution)/shard_map/reshape | solution.py:378
  2.0 0.7 stack.10
  2.6 0.7 stack.9
  3.3 0.1 copy.21.gb_ref
  3.5 0.0 copy-done
  3.5 0.1 reshape.22.f_ref
  3.7 0.0 copy-done.1
  3.7 0.1 reshape.23.d_ref
  3.8 63.3 %unit_backward.1 = (bf16[4,648,96]{2,1,0:T(8,128)(2,1)S(1)}, bf16[48,640]{1,0:T(8,128)(2,1)S(1)}) custom-call(bf16[48,640]{1,0:T(8,128)(2,1)S(1)} %reshape.22.f_ref, bf16[48,640]{1,0:T(8,128)(2,1)S(1)} %reshape.23.d_ref, bf16[3,384,216]{2,1,0:T(8,128)(2,1)S(1)} %copy.20.w_ref, f32[384,2]{1,0:T(8,128)S(1)} %copy.21.gb_ref), custom_call_target="tpu_custom_call" | custom-call | tf_op jit(solution)/shard_map/unit_backward/pallas_call | solution.py:382
  67.2 0.1 convert_bitcast_fusion
  67.3 0.3 copy.23
  67.6 1.6 %reshape.27 = f32[27,24,384]{2,1,0:T(8,128)} reshape(f32[648,4,96]{2,1,0:T(4,128)S(1)} %copy.23) | data formatting | bytes 1990656 | tf_op jit(solution)/shard_map/convert_element_type | solution.py:426
  69.2 0.1 reshape.26
  69.3 0.7 copy.25
  (3 shorter events, 0.1 us)
Async XLA Ops:
  0.6 2.9 %copy-start = (bf16[24,2,4,160]{3,2,1,0:T(4,128)(2,1)S(1)}, bf16[24,2,4,160]{3,2,1,0:T(4,128)(2,1)}, u32[]{:S(2)}) copy-start(bf16[24,2,4,160]{3,2,1,0:T(4,128)(2,1)} %param.5) | copy-start | bytes 184324
  0.6 3.0 %copy-start.1 = (bf16[24,2,4,160]{3,2,1,0:T(4,128)(2,1)S(1)}, bf16[24,2,4,160]{3,2,1,0:T(4,128)(2,1)}, u32[]{:S(2)}) copy-start(bf16[24,2,4,160]{3,2,1,0:T(4,128)(2,1)} %param.6) | copy-start | bytes 184324

commit v4 on v3

--- a/solution.py
+++ b/solution.py
@@ -39,11 +39,12 @@
 
 HALO = ((-1, 0), (0, 1), (0, -1), (-1, 1), (-1, -1))
 FIRST, FAR = 3 * 512, 512
-COPIES = 96
+COPIES = 112
+STEPS = tuple(slice(16 * n, 16 * n + 16) for n in range(3))
 
 
 def kernel(
-    f_ref, d_ref, w_ref, gb_ref, og_ref, od_ref,
+    f_ref, d_ref, raw_ref, gain_ref, bias_ref, og_ref, od_ref, wide, w_ref, gb_ref,
     dn, edges, fall, s9, p, pb, ry, q, qb, rz, actx, acty, inv, dacc,
     sown, smid, sry, srz, dsend, dmid, dry, drz, gc, first_bufs, far_bufs, ssem, rsem,
 ):
@@ -67,6 +68,7 @@
         for copy in copies:
             copy.wait_recv()
 
+    edges[...] = jnp.zeros_like(edges)
     barrier = pltpu.get_barrier_semaphore()
     greeted = [shifted(at, zh=1), shifted(at, zh=3)]
     greeted += [neighbour(at, -dx, -dh) for dx, dh in HALO]
@@ -81,17 +83,40 @@
     squares = squares * squares
     for t in range(2):
         sown[t : t + 1] = jnp.sum(squares[CH * t : CH * t + CH], axis=0, keepdims=True)
+    both = jnp.concatenate([gain_ref[...], bias_ref[...], jnp.zeros((6, TOTAL), F32)], axis=0)
+    gb_ref[...] = both.T
+
+    @pl.loop(0, CH)
+    def _(n):
+        whole = raw_ref[n].astype(F32)
+        for c in range(3):
+            wide[c, pl.ds(pl.multiple_of(n * 32, 32), 27)] = whole[:, 128 * c : 128 * c + 128]
+
+    for kt in range(3):
+        for c in range(3):
+            taps = [wide[c, pl.ds(9 * kt + j, CH, stride=32), :] for j in range(9)]
+            w_ref[kt, 128 * c : 128 * c + 128] = jnp.concatenate(taps, axis=0).T.astype(BF16)
+
     pl.semaphore_wait(barrier, len(greeted))
 
+    row = at["zl"] * 2 + at["k"]
+    below, above = row < 7, row > 0
+    frame = send(d_ref, dn, neighbour(at, -1, 0))
     halo = []
-    for n, (dx, dh) in enumerate(HALO):
-        if n == 0:
-            src, dst = d_ref, dn
-        else:
-            src = d_ref.at[:, pl.ds(384 if dh == 1 else 0, 256)]
-            dst = edges.at[n - 1]
-        halo.append(send(src, dst, neighbour(at, dx, dh)))
-    fz = [send(f_ref, fall.at[chan], shifted(at, zh=by)) for by in (1, 3)]
+    for n, (dx, dh) in enumerate(HALO[1:]):
+        i = count[0]
+        count[0] += 1
+        copy = pltpu.make_async_remote_copy(
+            src_ref=d_ref.at[:, pl.ds(384 if dh == 1 else 0, 256)], dst_ref=edges.at[n],
+            send_sem=ssem.at[i], recv_sem=rsem.at[i],
+            device_id=neighbour(at, dx, dh), device_id_type=MESH,
+        )
+        goes, comes = (below, above) if dh == 1 else (above, below)
+        pl.when(goes)(copy.start)
+        halo.append((copy, goes, comes))
+    fz = [
+        [send(f_ref.at[rows], fall.at[chan, rows], shifted(at, zh=by)) for by in (1, 3)] for rows in STEPS
+    ]
     sys = [send(sown, sry.at[by - 1], shifted(at, y=by)) for by in (2, 1, 3)]
 
     def forward(src, block):
@@ -99,19 +124,18 @@
 
     fy_own = forward(f_ref, chan)
 
-    arrived(halo)
+    arrived([frame])
+    for copy, _, comes in halo:
+        pl.when(comes)(copy.wait_recv)
     lane = lax.broadcasted_iota(jnp.int32, (CH, LANES), 1) % 160
     left_end, right_end = lane == 0, lane == 159
-    row = at["zl"] * 2 + at["k"]
-    top_on = jnp.where(row > 0, 1.0, 0.0).astype(F32)
-    bottom_on = jnp.where(row < 7, 1.0, 0.0).astype(F32)
     next_on = jnp.where(at["x"] < 3, 1.0, 0.0).astype(F32)
     for tp in range(4):
         rows = slice(CH * (tp % 2), CH * (tp % 2) + CH)
         late = tp >= 2
         own = (dn if late else d_ref)[...].astype(F32)[rows]
-        top = edges[2 if late else 0].astype(F32)[rows] * top_on
-        bottom = edges[3 if late else 1].astype(F32)[rows] * bottom_on
+        top = edges[2 if late else 0].astype(F32)[rows]
+        bottom = edges[3 if late else 1].astype(F32)[rows]
         if late:
             own, top, bottom = own * next_on, top * next_on, bottom * next_on
         moved = (
@@ -126,9 +150,20 @@
             pieces.append(jnp.where(left_end, 0.0, pltpu.roll(one, 1, 1)))
         s9[tp] = jnp.concatenate(pieces, axis=0).astype(BF16)
 
+    side = 1 + 2 * at["k"]
+    source = (at["zh"] + side) % 4 * 4 + at["y"]
+    away = {"tm": at["x"], "height": row, "chan": (at["zh"] + 4 - side) % 4 * 4 + at["y"]}
+    fz_far = []
+
+    def far_step(n):
+        arrived(fz[n])
+        ref = fall.at[source, STEPS[n]]
+        fz_far.append(send(ref, ref, away))
+
     arrived(sys)
     smid[0] = sown[...] + sry[0] + sry[1] + sry[2]
     szs = [send(smid.at[0], smid.at[by], shifted(at, zh=by)) for by in (1, 3)]
+    far_step(0)
 
     for t in range(2):
         total = None
@@ -137,6 +172,8 @@
             total = part if total is None else total + part
         p[t] = total
 
+    far_step(1)
+
     def parts(zh, y):
         start = pl.multiple_of((zh * 4 + y) * CH, 8)
         return jnp.concatenate([p[0, pl.ds(start, CH)], p[1, pl.ds(start, CH)]], axis=0)
@@ -153,15 +190,8 @@
     def block_at(by):
         return (at["zh"] + by) % 4 * 4 + at["y"]
 
-    side = 1 + 2 * at["k"]
-    arrived(fz)
-    source = (at["zh"] + side) % 4 * 4 + at["y"]
-    away = {"tm": at["x"], "height": row, "chan": (at["zh"] + 4 - side) % 4 * 4 + at["y"]}
-    fz_far = send(fall.at[source], fall.at[source], away)
+    far_step(2)
     fy_near = forward(fall.at[block_at(3)], block_at(3)) + forward(fall.at[block_at(1)], block_at(1))
-    reduce_y(1)
-    reduce_y(3)
-    reduce_y(0)
 
     arrived(szs)
     szf = send(smid.at[1], srz, shifted(at, zh=1))
@@ -175,7 +205,7 @@
         gain = gb_ref[pl.ds(start, CH), 0:1]
         bias = gb_ref[pl.ds(start, CH), 1:2]
         normed = x * inv[t : t + 1] * gain + bias
-        sig = 1.0 / (1.0 + jnp.exp(-normed))
+        sig = 0.5 * jnp.tanh(0.5 * normed) + 0.5
         return normed * sig, sig * (1.0 + normed * (1.0 - sig)) * gain
 
     def activate(by, dst, base):
@@ -228,9 +258,15 @@
     arrived(fy_own)
     activate(0, actx, 0)
     weigh(actx, 0, first_g, 0)
+    fy_far = []
+    for n in range(3):
+        arrived([fz_far[n]])
+        ref = fall.at[block_at(2), STEPS[n]]
+        fy_far += [send(ref, ref, shifted(at, y=by)) for by in (2, 1, 3)]
+    reduce_y(1)
+    reduce_y(3)
+    reduce_y(0)
     reduce_z(2)
-    arrived([fz_far])
-    fy_far = forward(fall.at[block_at(2)], block_at(2))
 
     def core_reduce(bufs, size):
         g, gr = bufs[0], bufs[1]
@@ -356,6 +392,8 @@
     deliver(far_bufs, 0, 2)
     for copy in started:
         copy.wait_send()
+    for copy, goes, _ in halo:
+        pl.when(goes)(copy.wait_send)
 
 
 def chain_buffers(size):
@@ -375,8 +413,6 @@
     chans, frames, rows, cols = features.shape
     f = jnp.transpose(features, (1, 0, 2, 3)).reshape(frames * chans, rows * cols)
     d = jnp.transpose(cotangent, (1, 0, 2, 3)).reshape(frames * chans, rows * cols)
-    w = jnp.transpose(conv_weight.reshape(chans, 3, 9, TOTAL), (1, 3, 2, 0)).reshape(3, TOTAL, 9 * chans)
-    gb = jnp.stack([norm_gain, norm_bias], axis=1)
     vmem = pl.BlockSpec(memory_space=pltpu.VMEM)
     sums = pltpu.VMEM((2, LANES), F32)
     grads, out = pl.pallas_call(
@@ -386,9 +422,12 @@
             jax.ShapeDtypeStruct((4, 648, 96), BF16),
             jax.ShapeDtypeStruct((48, LANES), BF16),
         ),
-        in_specs=[vmem] * 4,
+        in_specs=[vmem] * 5,
         out_specs=(vmem, vmem),
         scratch_shapes=[
+            pltpu.VMEM((3, CH * 32, 128), F32),
+            pltpu.VMEM((3, TOTAL, 9 * CH), BF16),
+            pltpu.VMEM((TOTAL, 8), F32),
             pltpu.VMEM((48, LANES), BF16),
             pltpu.VMEM((4, 48, 256), BF16),
             pltpu.VMEM((16, 48, LANES), BF16),
@@ -420,7 +459,7 @@
         compiler_params=pltpu.CompilerParams(
             collective_id=0, has_side_effects=True, vmem_limit_bytes=40 << 20
         ),
-    )(f, d, w, gb)
+    )(f, d, conv_weight, norm_gain.reshape(1, TOTAL), norm_bias.reshape(1, TOTAL))
     result = jnp.transpose(out.reshape(frames, chans, rows, cols), (1, 0, 2, 3))
     flat = jnp.transpose(grads, (1, 0, 2)).reshape(27, chans, TOTAL)
     weight_grad = jnp.transpose(flat, (1, 0, 2)).astype(F32)

time: 70.2 us -> 70.7 us (level)
  Pallas kernels: 63.3 us -> 64.6 us
  local copies, waits for them, and re-layouts: 5.85 us -> 5.11 us
    another operation x3 -> x0, local copies, waits for them, and re-layouts: 1.51 us -> none  [on_device(): gb = jnp.stack([norm_gain, norm_bias], axis=1)]
    reshape x1 -> x2, local copies, waits for them, and re-layouts: 1.31 us -> 0.01 us  [the longest x1 0.01 us: on_device(): norm_gain.reshape(1, TOTAL)]
    pallas_call x1, Pallas kernels: 63.3 us -> 64.6 us  [on_device(): pl.pallas_call(kernel, name='unit_backward', out_shape=(jax.ShapeDtypeStr...]
    unnamed x4 -> x7, local copies, waits for them, and re-layouts: 0.01 us -> 1.17 us
    transpose x1, local copies, waits for them, and re-layouts: 0.04 us -> 0.93 us  [on_device(): jnp.transpose(features, (1, 0, 2, 3)).reshape(frames * chans, rows * cols)]
where the time goes in v4:
time: 70.7 us; the launch traced here: 70.5 us
  Pallas kernels  64.6 us (91%)
  local copies, waits for them, and re-layouts  5.11 us (7%)
  between operations  0.75 us (1%)
    pallas_call x1, Pallas kernels, on_device(): pl.pallas_call(kernel, name='unit_backward', out_shape=(jax.ShapeDtypeStr...  64.6 us
    convert_element_type x2, local copies, waits for them, and re-layouts, on_device(): weight_grad = jnp.transpose(flat, (1, 0, 2)).astype(F32)  1.93 us

profile of v4, /device:TPU:1, one launch (start us, length us, event | category | flops | bytes accessed | tf_op | source)
XLA Modules:
  0.0 70.5 jit_solution(18195996864272389830)
XLA Ops:
  0.6 0.0 copy-start
  0.6 0.0 copy-start.1
  0.7 0.0 copy-start.2
  0.7 1.2 %copy.13.raw_ref = bf16[24,27,384]{2,1,0:T(8,128)(2,1)S(1)} copy(bf16[24,27,384]{2,0,1:T(8,128)(2,1)} %param.7) | data formatting | bytes 995328 | tf_op args[2]
  1.8 0.9 %copy.11 = bf16[2,24,4,160]{3,2,1,0:T(4,128)(2,1)S(1)} copy(bf16[2,24,4,160]{3,2,0,1:T(4,128)(2,1)} %bitcast.9) | data formatting | bytes 122880 | tf_op jit(solution)/shard_map/transpose | solution.py:414
  2.8 0.1 reshape.22.f_ref
  2.9 0.0 copy-done
  2.9 0.1 reshape.23.d_ref
  3.1 0.0 copy-done.1
  3.1 0.0 copy-done.2
  3.1 64.6 %unit_backward.1 = (bf16[4,648,96]{2,1,0:T(8,128)(2,1)S(1)}, bf16[48,640]{1,0:T(8,128)(2,1)S(1)}) custom-call(bf16[48,640]{1,0:T(8,128)(2,1)S(1)} %reshape.22.f_ref, bf16[48,640]{1,0:T(8,128)(2,1)S(1)} %reshape.23.d_ref, bf16[24,27,384]{2,1,0:T(8,128)(2,1)S(1)} %copy.13.raw_ref, f32[1,384]{1,0:T(1,128)S(1)} %reshape.24.gain_ref, f32[1,384]{1,0:T(1,128)S(1)} %reshape.25.bias_ref), custom_call_target="tpu_custom_call" | custom-call | tf_op jit(solution)/shard_map/unit_backward/pallas_call | solution.py:418
  67.7 0.1 convert_bitcast_fusion
  67.8 0.3 copy.15
  68.1 1.6 %reshape.27 = f32[27,24,384]{2,1,0:T(8,128)} reshape(f32[648,4,96]{2,1,0:T(4,128)S(1)} %copy.15) | data formatting | bytes 1990656 | tf_op jit(solution)/shard_map/convert_element_type | solution.py:465
  69.7 0.1 reshape.26
  69.8 0.7 copy.17
  (3 shorter events, 0.0 us)
Async XLA Ops:
  0.6 2.3 %copy-start = (bf16[24,2,4,160]{3,2,1,0:T(4,128)(2,1)S(1)}, bf16[24,2,4,160]{3,2,1,0:T(4,128)(2,1)}, u32[]{:S(2)}) copy-start(bf16[24,2,4,160]{3,2,1,0:T(4,128)(2,1)} %param.6) | copy-start | bytes 184324
  0.6 2.4 %copy-start.1 = (f32[384]{0:T(512)S(1)}, f32[384]{0:T(512)}, u32[]{:S(2)}) copy-start(f32[384]{0:T(512)} %param.8) | copy-start | bytes 4612
  0.7 2.4 %copy-start.2 = (f32[384]{0:T(512)S(1)}, f32[384]{0:T(512)}, u32[]{:S(2)}) copy-start(f32[384]{0:T(512)} %param.9) | copy-start | bytes 4612

commit v5 on v4

v5 whole, which is shorter than its diff:
```python
import functools
import math

import jax
import jax.numpy as jnp
from jax import lax
from jax.experimental import pallas as pl
from jax.experimental.pallas import tpu as pltpu
from jax.sharding import PartitionSpec as P

MESH = pl.DeviceIdType.MESH
SIZES = {"x": 4, "zl": 4, "k": 2, "zh": 4, "y": 4}
CH = 24
TOTAL = 384
LANES = 640
F32 = jnp.float32
BF16 = jnp.bfloat16


def coords():
    t = lax.axis_index("tm")
    h = lax.axis_index("height")
    c = lax.axis_index("chan")
    return {"x": t, "zl": h // 2, "k": h % 2, "zh": c // 4, "y": c % 4}


def shifted(at, **offsets):
    at = dict(at)
    for name, by in offsets.items():
        at[name] = (at[name] + (by % SIZES[name])) % SIZES[name]
    return {"tm": at["x"], "height": at["zl"] * 2 + at["k"], "chan": at["zh"] * 4 + at["y"]}


def neighbour(at, dx, dh):
    t = (at["x"] + (dx % 4)) % 4
    h = (at["zl"] * 2 + at["k"] + (dh % 8)) % 8
    return {"tm": t, "height": h, "chan": at["zh"] * 4 + at["y"]}


HALO = ((-1, 0), (0, 1), (0, -1), (-1, 1), (-1, -1))
COPIES = 96
STEPS = tuple(slice(16 * n, 16 * n + 16) for n in range(3))
SLOTS = (0, 1, 3, 2)
ROWS = 512
USED = 496


def kernel(
    f_ref, d_ref, raw_hbm, gain_ref, bias_ref, og_ref, od_ref,
    raw, wide, tall, slabs, wall, gb_ref, dall, dnall, edall, fall, s9, p, q, qb, rz, act, sx, inv,
    sown, smid, sry, srz, dsend, dmid, dry, drz, gc, perm, ag, chain_a, chain_b, lsem, ssem, rsem,
):
    at = coords()
    count = [0]
    started = []

    def send(src, dst, target):
        i = count[0]
        count[0] += 1
        copy = pltpu.make_async_remote_copy(
            src_ref=src, dst_ref=dst, send_sem=ssem.at[i], recv_sem=rsem.at[i],
            device_id=target, device_id_type=MESH,
        )
        copy.start()
        started.append(copy)
        return copy

    def arrived(copies):
        for copy in copies:
            copy.wait_recv()

    own_weight = pltpu.make_async_copy(raw_hbm, raw, lsem)
    own_weight.start()
    edall[0] = jnp.zeros((4, 48, 256), BF16)
    barrier = pltpu.get_barrier_semaphore()
    greeted = [shifted(at, zh=1), shifted(at, zh=3)]
    greeted += [neighbour(at, -dx, -dh) for dx, dh in HALO]
    greeted += [shifted(at, x=by) for by in (1, 2, 3)]
    greeted += [shifted(at, y=dy, zl=dz) for dy in range(4) for dz in range(4) if dy or dz]
    greeted.append(shifted(at, k=1))
    for one in greeted:
        pl.semaphore_signal(barrier, inc=1, device_id=one, device_id_type=MESH)

    fall[at["zh"]] = f_ref[...]
    squares = f_ref[...].astype(F32)
    squares = squares * squares
    for t in range(2):
        sown[t : t + 1] = jnp.sum(squares[CH * t : CH * t + CH], axis=0, keepdims=True)
    both = jnp.concatenate([gain_ref[...], bias_ref[...], jnp.zeros((6, TOTAL), F32)], axis=0)
    gb_ref[...] = both.T

    own_weight.wait()

    @pl.loop(0, CH)
    def _(n):
        whole = raw[n].astype(F32)
        for c in range(3):
            wide[c, pl.ds(pl.multiple_of(n * 32, 32), 27)] = whole[:, 128 * c : 128 * c + 128]

    for kt in range(3):
        for c in range(3):
            taps = [wide[c, pl.ds(9 * kt + j, CH, stride=32), :] for j in range(9)]
            tall[kt, 128 * c : 128 * c + 128] = jnp.concatenate(taps, axis=0).T

    def slab(by):
        y = (at["y"] + by) % 4
        groups = [
            tall[kt, pl.ds(pl.multiple_of(96 * zh + y * CH, 8), CH)] for kt in range(3) for zh in range(4)
        ]
        return jnp.concatenate(groups, axis=0).astype(BF16)

    wall[0] = slab(0)
    for by in (1, 2, 3):
        slabs[by - 1] = slab(by)
    r = lax.broadcasted_iota(jnp.int32, (96, TOTAL), 0)
    lane = lax.broadcasted_iota(jnp.int32, (96, TOTAL), 1)
    group = (r >= 24).astype(jnp.int32) + (r >= 48).astype(jnp.int32) + (r >= 72).astype(jnp.int32)
    for s in range(4):
        target = r + 72 * group + CH * ((at["y"] + s) % 4)
        perm[s] = jnp.where(lane == target, 1.0, 0.0).astype(BF16)

    pl.semaphore_wait(barrier, len(greeted))

    row = at["zl"] * 2 + at["k"]
    below, above = row < 7, row > 0
    frame = send(d_ref, dnall.at[0], neighbour(at, -1, 0))
    halo = []
    for n, (dx, dh) in enumerate(HALO[1:]):
        i = count[0]
        count[0] += 1
        copy = pltpu.make_async_remote_copy(
            src_ref=d_ref.at[:, pl.ds(384 if dh == 1 else 0, 256)], dst_ref=edall.at[0, n],
            send_sem=ssem.at[i], recv_sem=rsem.at[i],
            device_id=neighbour(at, dx, dh), device_id_type=MESH,
        )
        goes, comes = (below, above) if dh == 1 else (above, below)
        pl.when(goes)(copy.start)
        halo.append((copy, goes, comes))
    fz = [
        [send(f_ref.at[rows], fall.at[at["zh"], rows], shifted(at, zh=by)) for by in (1, 3)] for rows in STEPS
    ]
    sys = [send(sown, sry.at[by - 1], shifted(at, y=by)) for by in (2, 1, 3)]
    dy = {by: [send(d_ref, dall.at[by - 1], shifted(at, y=by))] for by in (2, 1, 3)}

    arrived([frame])
    for by in (2, 1, 3):
        dy[by].append(send(dnall.at[0], dnall.at[by], shifted(at, y=by)))
    for copy, _, comes in halo:
        pl.when(comes)(copy.wait_recv)
    for by in (2, 1, 3):
        dy[by].append(send(edall.at[0], edall.at[by], shifted(at, y=by)))
    half = pl.multiple_of(at["k"] * 144, 16)
    ws = [
        send(slabs.at[by - 1, pl.ds(half, 144)], wall.at[by, pl.ds(half, 144)], shifted(at, y=by))
        for by in (2, 1, 3)
    ]

    column = lax.broadcasted_iota(jnp.int32, (CH, LANES), 1) % 160
    left_end, right_end = column == 0, column == 159
    next_on = jnp.where(at["x"] < 3, 1.0, 0.0).astype(F32)

    def build(slot):
        for tp in range(4):
            rows = slice(CH * (tp % 2), CH * (tp % 2) + CH)
            late = tp >= 2
            if late:
                own = dnall[slot].astype(F32)[rows]
            else:
                own = (d_ref[...] if slot == 0 else dall[slot - 1]).astype(F32)[rows]
            top = edall[slot, 2 if late else 0].astype(F32)[rows]
            bottom = edall[slot, 3 if late else 1].astype(F32)[rows]
            if late:
                own, top, bottom = own * next_on, top * next_on, bottom * next_on
            moved = (
                jnp.concatenate([own[:, 160:], bottom[:, :160]], axis=1),
                own,
                jnp.concatenate([top[:, 96:], own[:, :480]], axis=1),
            )
            pieces = []
            for one in moved:
                pieces.append(jnp.where(right_end, 0.0, pltpu.roll(one, LANES - 1, 1)))
                pieces.append(one)
                pieces.append(jnp.where(left_end, 0.0, pltpu.roll(one, 1, 1)))
            s9[slot, tp] = jnp.concatenate(pieces, axis=0).astype(BF16)

    side = 1 + 2 * at["k"]
    source = (at["zh"] + side) % 4
    away = {"tm": at["x"], "height": row, "chan": (at["zh"] + 4 - side) % 4 * 4 + at["y"]}
    fz_far = []

    def far_step(n):
        arrived(fz[n])
        ref = fall.at[source, STEPS[n]]
        fz_far.append(send(ref, ref, away))

    arrived(sys)
    smid[0] = sown[...] + sry[0] + sry[1] + sry[2]
    szs = [send(smid.at[0], smid.at[by], shifted(at, zh=by)) for by in (1, 3)]
    far_step(0)
    build(0)
    far_step(1)
    far_step(2)
    arrived(szs)
    szf = send(smid.at[1], srz, shifted(at, zh=1))
    for by in (1, 3, 2):
        arrived(dy[by])
        build(by)

    arrived([szf])
    total = smid[0] + smid[1] + smid[3] + srz[...]
    inv[...] = lax.rsqrt(total * (1.0 / TOTAL) + 1e-06)

    def activation(x, t, block):
        start = pl.multiple_of(block * CH, 8)
        gain = gb_ref[pl.ds(start, CH), 0:1]
        bias = gb_ref[pl.ds(start, CH), 1:2]
        normed = x * inv[t : t + 1] * gain + bias
        sig = 0.5 * jnp.tanh(0.5 * normed) + 0.5
        return normed * sig, sig * (1.0 + normed * (1.0 - sig)) * gain

    arrived(fz_far)

    @pl.loop(0, 2)
    def _(n):
        blocks = [fall[2 * n + j].astype(F32) for j in range(2)]
        for t in range(2):
            pair, slopes = [], []
            for j in range(2):
                x = blocks[j][CH * t : CH * t + CH]
                active, slope = activation(x, t, (2 * n + j) * 4 + at["y"])
                pair.append(active)
                slopes.append(slope * x)
            start = pl.multiple_of(n * 48, 16)
            act[t, pl.ds(start, 48)] = jnp.concatenate(pair, axis=0).astype(BF16)
            sx[t, pl.ds(start, 48)] = jnp.concatenate(slopes, axis=0)

    def weigh(slot, g, n):
        for kt in range(3):
            total = None
            for t in range(2):
                part = lax.dot_general(
                    s9[slot, t + 2 - kt], act[t], (((1,), (1,)), ((), ())), preferred_element_type=F32
                )
                total = part if total is None else total + part
            gc[216 * kt : 216 * kt + 216] = total
        g[n, 0:328] = jnp.concatenate([gc[0:328, 0:64], gc[320:648, 0:64]], axis=1)
        g[n, 328:USED] = jnp.concatenate([gc[160 * m : 160 * m + 168, 64:96] for m in range(4)], axis=1)
        g[n, USED:ROWS] = jnp.zeros((ROWS - USED, 128), F32)

    def core_reduce(bufs):
        other = pl.multiple_of((1 - at["k"]) * 256, 256)
        return send(bufs[0].at[:, pl.ds(other, 256)], bufs[1], shifted(at, k=1))

    def x_reduce(bufs):
        g, gr, h, hb, hr = bufs[:5]
        sends = []
        for by in (2, 1, 3, 0):
            start = (at["x"] + by) % 4 * 64
            value = (
                g[:, pl.ds(pl.multiple_of(at["k"] * 256 + start, 64), 64)]
                + gr[:, pl.ds(pl.multiple_of(start, 64), 64)]
            )
            if by == 0:
                h[...] = value
            else:
                hb[by - 1] = value.astype(BF16)
                sends.append(send(hb.at[by - 1], hr.at[by - 1], shifted(at, x=by)))
        return sends

    def z_reduce(bufs):
        h, hr, zs, zr = bufs[2], bufs[4], bufs[5], bufs[6]
        h[...] = h[...] + hr[0].astype(F32) + hr[1].astype(F32) + hr[2].astype(F32)
        sends = []
        for by in (3, 1, 2):
            zs[by - 1] = h[:, pl.ds(pl.multiple_of((at["zl"] + by) % 4 * 16, 16), 16)]
            sends.append(send(zs.at[by - 1], zr.at[by - 1], shifted(at, zl=by)))
        return sends

    def yz_gather(bufs, base):
        h, zr, sb = bufs[2], bufs[6], bufs[7]
        value = h[:, pl.ds(pl.multiple_of(at["zl"] * 16, 16), 16)] + zr[0] + zr[1] + zr[2]
        sb[...] = (value * (1.0 / math.sqrt(40960))).astype(BF16)
        piece = pl.multiple_of(at["k"] * 256 + at["x"] * 64 + at["zl"] * 16, 16)
        sends = []
        for n in range(2):
            slot = SLOTS[base + n]
            for dz in (3, 2, 1, 0):
                if slot == 0 and dz == 0:
                    ag[0, pl.ds(piece, 16)] = sb[0]
                else:
                    dst = ag.at[base + n, pl.ds(piece, 16)]
                    sends.append(send(sb.at[n], dst, shifted(at, y=-slot, zl=dz)))
        return sends

    def x_gather(base):
        start = pl.multiple_of(at["k"] * 256 + at["x"] * 64, 64)
        ref = ag.at[pl.ds(base, 2), pl.ds(start, 64)]
        return [send(ref, ref, shifted(at, x=by)) for by in (2, 1, 3)]

    def core_gather(base):
        ref = ag.at[pl.ds(base, 2), pl.ds(pl.multiple_of(at["k"] * 256, 256), 256)]
        return send(ref, ref, shifted(at, k=1))

    def unpack(place):
        value = ag[place].astype(F32)
        low, high = value[:328], value[328:USED]
        left = jnp.concatenate([low[:, :64], low[8:, 64:]], axis=0)
        right = jnp.concatenate(
            [high[:, :32], high[8:, 32:64], high[8:, 64:96], high[8:, 96:]], axis=0
        )
        piece = jnp.concatenate([left, right], axis=1).astype(BF16)
        return jnp.dot(piece, perm[SLOTS[place]], preferred_element_type=F32)

    weigh(SLOTS[0], chain_a[0], 0)
    weigh(SLOTS[1], chain_a[0], 1)
    a = core_reduce(chain_a)
    arrived(ws)
    ref = wall.at[pl.ds(1, 3), pl.ds(half, 144)]
    wx = send(ref, ref, shifted(at, k=1))
    weigh(SLOTS[2], chain_b[0], 0)
    weigh(SLOTS[3], chain_b[0], 1)
    b = core_reduce(chain_b)
    arrived([a])
    a = x_reduce(chain_a)
    arrived([wx])
    for tp, (low, high) in enumerate(((192, 288), (96, 288), (0, 192), (0, 96))):
        total = None
        for slot in range(4):
            part = jnp.dot(wall[slot, low:high], s9[slot, tp], preferred_element_type=F32)
            total = part if total is None else total + part
        if tp == 0:
            p[0] = total
        elif tp == 1:
            p[0] += total[:96]
            p[1] = total[96:]
        elif tp == 2:
            p[0] += total[:96]
            p[1] += total[96:]
        else:
            p[1] += total

    arrived([b])
    b = x_reduce(chain_b)
    zsends = []
    for by in (2, 1, 3, 0):
        start = pl.multiple_of((at["zh"] + by) % 4 * CH, 8)
        value = jnp.concatenate([p[0, pl.ds(start, CH)], p[1, pl.ds(start, CH)]], axis=0)
        if by == 0:
            q[...] = value
        else:
            qb[by - 1] = value.astype(BF16)
            zsends.append(send(qb.at[by - 1], rz.at[by - 1], shifted(at, zh=by)))
    for t in range(2):
        dsend[t : t + 1] = jnp.sum(p[t] * sx[t], axis=0, keepdims=True)
    dys = [send(dsend, dry.at[by - 1], shifted(at, y=by)) for by in (2, 1, 3)]
    arrived(a)
    a = z_reduce(chain_a)
    arrived(b)
    b = z_reduce(chain_b)
    arrived(dys)
    dmid[...] = dsend[...] + dry[0] + dry[1] + dry[2]
    dzs = [send(dmid, drz.at[by - 1], shifted(at, zh=by)) for by in (2, 1, 3)]
    arrived(a)
    a = yz_gather(chain_a, 0)
    arrived(b)
    b = yz_gather(chain_b, 2)
    arrived(a)
    a = x_gather(0)
    arrived(b)
    b = x_gather(2)
    arrived(a)
    a = core_gather(0)
    arrived(b)
    b = core_gather(2)

    arrived(zsends + dzs)
    grad = q[...] + rz[0].astype(F32) + rz[1].astype(F32) + rz[2].astype(F32)
    dots = dmid[...] + drz[0] + drz[1] + drz[2]
    mine_x = f_ref[...].astype(F32)
    ct = d_ref[...].astype(F32)
    outs = []
    for t in range(2):
        rows = slice(CH * t, CH * t + CH)
        x = mine_x[rows]
        _, slope = activation(x, t, at["zh"] * 4 + at["y"])
        up = grad[rows] * slope
        r = inv[t : t + 1]
        back = r * up - x * (r * r * r * dots[t : t + 1] * (1.0 / TOTAL))
        outs.append(ct[rows] + back)
    od_ref[...] = jnp.concatenate(outs, axis=0).astype(BF16)

    arrived([a, b])
    og_ref[...] = (unpack(0) + unpack(1) + unpack(2) + unpack(3)).astype(BF16)
    for copy in started:
        copy.wait_send()
    for copy, goes, _ in halo:
        pl.when(goes)(copy.wait_send)


def chain_buffers():
    return [
        pltpu.VMEM((2, ROWS, 128), F32),
        pltpu.VMEM((2, 256, 128), F32),
        pltpu.VMEM((2, 64, 128), F32),
        pltpu.VMEM((3, 2, 64, 128), BF16),
        pltpu.VMEM((3, 2, 64, 128), BF16),
        pltpu.VMEM((3, 2, 16, 128), F32),
        pltpu.VMEM((3, 2, 16, 128), F32),
        pltpu.VMEM((2, 16, 128), BF16),
    ]


def on_device(features, cotangent, conv_weight, norm_gain, norm_bias):
    chans, frames, rows, cols = features.shape
    f = jnp.transpose(features, (1, 0, 2, 3)).reshape(frames * chans, rows * cols)
    d = jnp.transpose(cotangent, (1, 0, 2, 3)).reshape(frames * chans, rows * cols)
    vmem = pl.BlockSpec(memory_space=pltpu.VMEM)
    sums = pltpu.VMEM((2, LANES), F32)
    sums3 = pltpu.VMEM((3, 2, LANES), F32)
    cells = pltpu.VMEM((3, 48, LANES), BF16)
    grads, out = pl.pallas_call(
        kernel,
        name="unit_backward",
        out_shape=(
            jax.ShapeDtypeStruct((648, TOTAL), BF16),
            jax.ShapeDtypeStruct((48, LANES), BF16),
        ),
        in_specs=[vmem, vmem, pl.BlockSpec(memory_space=pl.ANY), vmem, vmem],
        out_specs=(vmem, vmem),
        scratch_shapes=[
            pltpu.VMEM((CH, 27, TOTAL), BF16),
            pltpu.VMEM((3, CH * 32, 128), F32),
            pltpu.VMEM((3, TOTAL, 9 * CH), F32),
            pltpu.VMEM((3, 288, 9 * CH), BF16),
            pltpu.VMEM((4, 288, 9 * CH), BF16),
            pltpu.VMEM((TOTAL, 8), F32),
            cells,
            pltpu.VMEM((4, 48, LANES), BF16),
            pltpu.VMEM((4, 4, 48, 256), BF16),
            pltpu.VMEM((4, 48, LANES), BF16),
            pltpu.VMEM((4, 4, 216, LANES), BF16),
            pltpu.VMEM((2, 96, LANES), F32),
            pltpu.VMEM((48, LANES), F32),
            cells,
            cells,
            pltpu.VMEM((2, 96, LANES), BF16),
            pltpu.VMEM((2, 96, LANES), F32),
            sums,
            sums,
            pltpu.VMEM((4, 2, LANES), F32),
            sums3,
            sums,
            sums,
            sums,
            sums3,
            sums3,
            pltpu.VMEM((648, 96), F32),
            pltpu.VMEM((4, 96, TOTAL), BF16),
            pltpu.VMEM((4, ROWS, 128), BF16),
            chain_buffers(),
            chain_buffers(),
            pltpu.SemaphoreType.DMA,
            pltpu.SemaphoreType.DMA((COPIES,)),
            pltpu.SemaphoreType.DMA((COPIES,)),
        ],
        compiler_params=pltpu.CompilerParams(
            collective_id=0, has_side_effects=True, vmem_limit_bytes=40 << 20
        ),
    )(f, d, conv_weight, norm_gain.reshape(1, TOTAL), norm_bias.reshape(1, TOTAL))
    result = jnp.transpose(out.reshape(frames, chans, rows, cols), (1, 0, 2, 3))
    weight_grad = jnp.transpose(grads.reshape(27, chans, TOTAL), (1, 0, 2)).astype(F32)
    return result, weight_grad


def solution(mesh):
    return jax.shard_map(
        on_device,
        mesh=mesh,
        in_specs=(
            P("chan", "tm", "height", None),
            P("chan", "tm", "height", None),
            P("chan", None, None),
            P(),
            P(),
        ),
        out_specs=(P("chan", "tm", "height", None), P("chan", None, None)),
        check_vma=False,
    )
```

time: 70.7 us -> 70.9 us (level)
  other arithmetic: 0.09 us -> 1.01 us
  local copies, waits for them, and re-layouts: 5.11 us -> 4.25 us
    unnamed x7 -> x9, local copies, waits for them, and re-layouts: 1.17 us -> 3.14 us
    convert_element_type x2 -> x0, local copies, waits for them, and re-layouts: 1.93 us -> none  [on_device(): weight_grad = jnp.transpose(flat, (1, 0, 2)).astype(F32)]
    convert_element_type x1, other arithmetic: 0.09 us -> 1.01 us  [on_device(): jnp.transpose(grads.reshape(27, chans, TOTAL), (1, 0, 2)).astype(F32)]
    transpose x1, local copies, waits for them, and re-layouts: 0.93 us -> 0.04 us  [on_device(): jnp.transpose(features, (1, 0, 2, 3)).reshape(frames * chans, rows * cols)]
where the time goes in v5:
time: 70.9 us; the launch traced here: 70.7 us
  Pallas kernels  64.7 us (91%)
  local copies, waits for them, and re-layouts  4.25 us (6%)
  other arithmetic  1.01 us (1%)
    pallas_call x1, Pallas kernels, on_device(): pl.pallas_call(kernel, name='unit_backward', out_shape=(jax.ShapeDtypeStr...  64.7 us
    unnamed x9, local copies, waits for them, and re-layouts  3.14 us

profile of v5, /device:TPU:1, one launch (start us, length us, event | category | flops | bytes accessed | tf_op | source)
XLA Modules:
  0.0 70.7 jit_solution(7696729818354838041)
XLA Ops:
  0.6 0.0 copy-start
  0.6 1.1 %copy.9.raw_hbm = bf16[24,27,384]{2,1,0:T(8,128)(2,1)S(1)} copy(bf16[24,27,384]{2,0,1:T(8,128)(2,1)} %param.7) | data formatting | bytes 995328 | tf_op args[2]
  1.8 0.0 copy-done
  1.8 0.0 copy-start.1
  1.9 0.1 reshape.22.f_ref
  2.0 0.8 %copy-done.1 = bf16[24,2,4,160]{3,2,1,0:T(4,128)(2,1)S(1)} copy-done((bf16[24,2,4,160]{3,2,1,0:T(4,128)(2,1)S(1)}, bf16[24,2,4,160]{3,2,1,0:T(4,128)(2,1)}, u32[]{:S(2)}) %copy-start.1) | copy-done | bytes 61464
  2.8 0.0 copy-start.2
  2.8 0.1 reshape.23.d_ref
  2.9 0.5 copy-done.2
  3.5 0.0 copy-start.3
  3.5 0.7 copy-done.3
  4.1 64.7 %unit_backward.1 = (bf16[648,384]{1,0:T(8,128)(2,1)S(1)}, bf16[48,640]{1,0:T(8,128)(2,1)S(1)}) custom-call(bf16[48,640]{1,0:T(8,128)(2,1)S(1)} %reshape.22.f_ref, bf16[48,640]{1,0:T(8,128)(2,1)S(1)} %reshape.23.d_ref, bf16[24,27,384]{2,1,0:T(8,128)(2,1)S(1)} %copy.9.raw_hbm, f32[1,384]{1,0:T(1,128)S(1)} %reshape.24.gain_ref, f32[1,384]{1,0:T(1,128)S(1)} %reshape.25.bias_ref), custom_call_target="tpu_custom_call" | custom-call | tf_op jit(solution)/shard_map/unit_backward/pallas_call | solution.py:421
  68.8 1.0 %convert_bitcast_fusion = f32[24,27,384]{2,0,1:T(8,128)} fusion(bf16[27,24,384]{2,1,0:T(8,128)(2,1)S(1)} %bitcast.9), kind=kLoop, calls=%fused_computation | loop fusion | flops 248832 | bytes 1492992 | tf_op jit(solution)/shard_map/convert_element_type | solution.py:471
  69.9 0.1 reshape.26
  70.0 0.7 copy.12
  (4 shorter events, 0.1 us)
Async XLA Ops:
  0.6 1.2 %copy-start = (bf16[24,2,4,160]{3,2,1,0:T(4,128)(2,1)S(1)}, bf16[24,2,4,160]{3,2,1,0:T(4,128)(2,1)}, u32[]{:S(2)}) copy-start(bf16[24,2,4,160]{3,2,1,0:T(4,128)(2,1)} %param.5) | copy-start | bytes 184324
  1.8 0.9 %copy-start.1 = (bf16[24,2,4,160]{3,2,1,0:T(4,128)(2,1)S(1)}, bf16[24,2,4,160]{3,2,1,0:T(4,128)(2,1)}, u32[]{:S(2)}) copy-start(bf16[24,2,4,160]{3,2,1,0:T(4,128)(2,1)} %param.6) | copy-start | bytes 184324
  2.8 0.7 copy-start.2
  3.5 0.7 copy-start.3

commit v6 on v5

--- a/solution.py
+++ b/solution.py
@@ -46,8 +46,8 @@
 
 
 def kernel(
-    f_ref, d_ref, raw_hbm, gain_ref, bias_ref, og_ref, od_ref,
-    raw, wide, tall, slabs, wall, gb_ref, dall, dnall, edall, fall, s9, p, q, qb, rz, act, sx, inv,
+    f_ref, d_ref, raw_hbm, gain_hbm, bias_hbm, og_ref, od_ref,
+    raw, gain_ref, bias_ref, tall, slabs, wall, gb_ref, dall, dnall, edall, fall, s9, p, q, qb, rz, act, sx, inv,
     sown, smid, sry, srz, dsend, dmid, dry, drz, gc, perm, ag, chain_a, chain_b, lsem, ssem, rsem,
 ):
     at = coords()
@@ -69,8 +69,12 @@
         for copy in copies:
             copy.wait_recv()
 
-    own_weight = pltpu.make_async_copy(raw_hbm, raw, lsem)
-    own_weight.start()
+    loads = [
+        pltpu.make_async_copy(src, dst, lsem.at[n])
+        for n, (src, dst) in enumerate(((gain_hbm, gain_ref), (bias_hbm, bias_ref), (raw_hbm, raw)))
+    ]
+    for copy in loads:
+        copy.start()
     edall[0] = jnp.zeros((4, 48, 256), BF16)
     barrier = pltpu.get_barrier_semaphore()
     greeted = [shifted(at, zh=1), shifted(at, zh=3)]
@@ -86,21 +90,15 @@
     squares = squares * squares
     for t in range(2):
         sown[t : t + 1] = jnp.sum(squares[CH * t : CH * t + CH], axis=0, keepdims=True)
-    both = jnp.concatenate([gain_ref[...], bias_ref[...], jnp.zeros((6, TOTAL), F32)], axis=0)
+    loads[0].wait()
+    loads[1].wait()
+    pair = [ref[...].reshape(1, TOTAL) for ref in (gain_ref, bias_ref)]
+    both = jnp.concatenate(pair + [jnp.zeros((6, TOTAL), F32)], axis=0)
     gb_ref[...] = both.T
 
-    own_weight.wait()
-
-    @pl.loop(0, CH)
-    def _(n):
-        whole = raw[n].astype(F32)
-        for c in range(3):
-            wide[c, pl.ds(pl.multiple_of(n * 32, 32), 27)] = whole[:, 128 * c : 128 * c + 128]
-
+    loads[2].wait()
     for kt in range(3):
-        for c in range(3):
-            taps = [wide[c, pl.ds(9 * kt + j, CH, stride=32), :] for j in range(9)]
-            tall[kt, 128 * c : 128 * c + 128] = jnp.concatenate(taps, axis=0).T
+        tall[kt] = raw[216 * kt : 216 * kt + 216].astype(F32).T
 
     def slab(by):
         y = (at["y"] + by) % 4
@@ -142,6 +140,12 @@
     sys = [send(sown, sry.at[by - 1], shifted(at, y=by)) for by in (2, 1, 3)]
     dy = {by: [send(d_ref, dall.at[by - 1], shifted(at, y=by))] for by in (2, 1, 3)}
 
+    half = pl.multiple_of(at["k"] * 144, 16)
+    ws = [
+        send(slabs.at[by - 1, pl.ds(half, 144)], wall.at[by, pl.ds(half, 144)], shifted(at, y=by))
+        for by in (2, 1, 3)
+    ]
+
     arrived([frame])
     for by in (2, 1, 3):
         dy[by].append(send(dnall.at[0], dnall.at[by], shifted(at, y=by)))
@@ -149,12 +153,6 @@
         pl.when(comes)(copy.wait_recv)
     for by in (2, 1, 3):
         dy[by].append(send(edall.at[0], edall.at[by], shifted(at, y=by)))
-    half = pl.multiple_of(at["k"] * 144, 16)
-    ws = [
-        send(slabs.at[by - 1, pl.ds(half, 144)], wall.at[by, pl.ds(half, 144)], shifted(at, y=by))
-        for by in (2, 1, 3)
-    ]
-
     column = lax.broadcasted_iota(jnp.int32, (CH, LANES), 1) % 160
     left_end, right_end = column == 0, column == 159
     next_on = jnp.where(at["x"] < 3, 1.0, 0.0).astype(F32)
@@ -200,128 +198,15 @@
     build(0)
     far_step(1)
     far_step(2)
+    arrived(ws)
+    ref = wall.at[pl.ds(1, 3), pl.ds(half, 144)]
+    wx = send(ref, ref, shifted(at, k=1))
     arrived(szs)
     szf = send(smid.at[1], srz, shifted(at, zh=1))
     for by in (1, 3, 2):
         arrived(dy[by])
         build(by)
 
-    arrived([szf])
-    total = smid[0] + smid[1] + smid[3] + srz[...]
-    inv[...] = lax.rsqrt(total * (1.0 / TOTAL) + 1e-06)
-
-    def activation(x, t, block):
-        start = pl.multiple_of(block * CH, 8)
-        gain = gb_ref[pl.ds(start, CH), 0:1]
-        bias = gb_ref[pl.ds(start, CH), 1:2]
-        normed = x * inv[t : t + 1] * gain + bias
-        sig = 0.5 * jnp.tanh(0.5 * normed) + 0.5
-        return normed * sig, sig * (1.0 + normed * (1.0 - sig)) * gain
-
-    arrived(fz_far)
-
-    @pl.loop(0, 2)
-    def _(n):
-        blocks = [fall[2 * n + j].astype(F32) for j in range(2)]
-        for t in range(2):
-            pair, slopes = [], []
-            for j in range(2):
-                x = blocks[j][CH * t : CH * t + CH]
-                active, slope = activation(x, t, (2 * n + j) * 4 + at["y"])
-                pair.append(active)
-                slopes.append(slope * x)
-            start = pl.multiple_of(n * 48, 16)
-            act[t, pl.ds(start, 48)] = jnp.concatenate(pair, axis=0).astype(BF16)
-            sx[t, pl.ds(start, 48)] = jnp.concatenate(slopes, axis=0)
-
-    def weigh(slot, g, n):
-        for kt in range(3):
-            total = None
-            for t in range(2):
-                part = lax.dot_general(
-                    s9[slot, t + 2 - kt], act[t], (((1,), (1,)), ((), ())), preferred_element_type=F32
-                )
-                total = part if total is None else total + part
-            gc[216 * kt : 216 * kt + 216] = total
-        g[n, 0:328] = jnp.concatenate([gc[0:328, 0:64], gc[320:648, 0:64]], axis=1)
-        g[n, 328:USED] = jnp.concatenate([gc[160 * m : 160 * m + 168, 64:96] for m in range(4)], axis=1)
-        g[n, USED:ROWS] = jnp.zeros((ROWS - USED, 128), F32)
-
-    def core_reduce(bufs):
-        other = pl.multiple_of((1 - at["k"]) * 256, 256)
-        return send(bufs[0].at[:, pl.ds(other, 256)], bufs[1], shifted(at, k=1))
-
-    def x_reduce(bufs):
-        g, gr, h, hb, hr = bufs[:5]
-        sends = []
-        for by in (2, 1, 3, 0):
-            start = (at["x"] + by) % 4 * 64
-            value = (
-                g[:, pl.ds(pl.multiple_of(at["k"] * 256 + start, 64), 64)]
-                + gr[:, pl.ds(pl.multiple_of(start, 64), 64)]
-            )
-            if by == 0:
-                h[...] = value
-            else:
-                hb[by - 1] = value.astype(BF16)
-                sends.append(send(hb.at[by - 1], hr.at[by - 1], shifted(at, x=by)))
-        return sends
-
-    def z_reduce(bufs):
-        h, hr, zs, zr = bufs[2], bufs[4], bufs[5], bufs[6]
-        h[...] = h[...] + hr[0].astype(F32) + hr[1].astype(F32) + hr[2].astype(F32)
-        sends = []
-        for by in (3, 1, 2):
-            zs[by - 1] = h[:, pl.ds(pl.multiple_of((at["zl"] + by) % 4 * 16, 16), 16)]
-            sends.append(send(zs.at[by - 1], zr.at[by - 1], shifted(at, zl=by)))
-        return sends
-
-    def yz_gather(bufs, base):
-        h, zr, sb = bufs[2], bufs[6], bufs[7]
-        value = h[:, pl.ds(pl.multiple_of(at["zl"] * 16, 16), 16)] + zr[0] + zr[1] + zr[2]
-        sb[...] = (value * (1.0 / math.sqrt(40960))).astype(BF16)
-        piece = pl.multiple_of(at["k"] * 256 + at["x"] * 64 + at["zl"] * 16, 16)
-        sends = []
-        for n in range(2):
-            slot = SLOTS[base + n]
-            for dz in (3, 2, 1, 0):
-                if slot == 0 and dz == 0:
-                    ag[0, pl.ds(piece, 16)] = sb[0]
-                else:
-                    dst = ag.at[base + n, pl.ds(piece, 16)]
-                    sends.append(send(sb.at[n], dst, shifted(at, y=-slot, zl=dz)))
-        return sends
-
-    def x_gather(base):
-        start = pl.multiple_of(at["k"] * 256 + at["x"] * 64, 64)
-        ref = ag.at[pl.ds(base, 2), pl.ds(start, 64)]
-        return [send(ref, ref, shifted(at, x=by)) for by in (2, 1, 3)]
-
-    def core_gather(base):
-        ref = ag.at[pl.ds(base, 2), pl.ds(pl.multiple_of(at["k"] * 256, 256), 256)]
-        return send(ref, ref, shifted(at, k=1))
-
-    def unpack(place):
-        value = ag[place].astype(F32)
-        low, high = value[:328], value[328:USED]
-        left = jnp.concatenate([low[:, :64], low[8:, 64:]], axis=0)
-        right = jnp.concatenate(
-            [high[:, :32], high[8:, 32:64], high[8:, 64:96], high[8:, 96:]], axis=0
-        )
-        piece = jnp.concatenate([left, right], axis=1).astype(BF16)
-        return jnp.dot(piece, perm[SLOTS[place]], preferred_element_type=F32)
-
-    weigh(SLOTS[0], chain_a[0], 0)
-    weigh(SLOTS[1], chain_a[0], 1)
-    a = core_reduce(chain_a)
-    arrived(ws)
-    ref = wall.at[pl.ds(1, 3), pl.ds(half, 144)]
-    wx = send(ref, ref, shifted(at, k=1))
-    weigh(SLOTS[2], chain_b[0], 0)
-    weigh(SLOTS[3], chain_b[0], 1)
-    b = core_reduce(chain_b)
-    arrived([a])
-    a = x_reduce(chain_a)
     arrived([wx])
     for tp, (low, high) in enumerate(((192, 288), (96, 288), (0, 192), (0, 96))):
         total = None
@@ -339,8 +224,6 @@
         else:
             p[1] += total
 
-    arrived([b])
-    b = x_reduce(chain_b)
     zsends = []
     for by in (2, 1, 3, 0):
         start = pl.multiple_of((at["zh"] + by) % 4 * CH, 8)
@@ -350,16 +233,131 @@
         else:
             qb[by - 1] = value.astype(BF16)
             zsends.append(send(qb.at[by - 1], rz.at[by - 1], shifted(at, zh=by)))
+    arrived([szf])
+    total = smid[0] + smid[1] + smid[3] + srz[...]
+    inv[...] = lax.rsqrt(total * (1.0 / TOTAL) + 1e-06)
+
+    def activation(x, t, block):
+        start = pl.multiple_of(block * CH, 8)
+        gain = gb_ref[pl.ds(start, CH), 0:1]
+        bias = gb_ref[pl.ds(start, CH), 1:2]
+        normed = x * inv[t : t + 1] * gain + bias
+        sig = 0.5 * jnp.tanh(0.5 * normed) + 0.5
+        return normed * sig, sig * (1.0 + normed * (1.0 - sig)) * gain
+
+    arrived(fz_far)
+
+    @pl.loop(0, 2)
+    def _(n):
+        blocks = [fall[2 * n + j].astype(F32) for j in range(2)]
+        for t in range(2):
+            pair, slopes = [], []
+            for j in range(2):
+                x = blocks[j][CH * t : CH * t + CH]
+                active, slope = activation(x, t, (2 * n + j) * 4 + at["y"])
+                pair.append(active)
+                slopes.append(slope * x)
+            start = pl.multiple_of(n * 48, 16)
+            act[t, pl.ds(start, 48)] = jnp.concatenate(pair, axis=0).astype(BF16)
+            sx[t, pl.ds(start, 48)] = jnp.concatenate(slopes, axis=0)
+
+    def weigh(slot, g, n):
+        for kt in range(3):
+            total = None
+            for t in range(2):
+                part = lax.dot_general(
+                    s9[slot, t + 2 - kt], act[t], (((1,), (1,)), ((), ())), preferred_element_type=F32
+                )
+                total = part if total is None else total + part
+            gc[216 * kt : 216 * kt + 216] = total
+        g[n, 0:328] = jnp.concatenate([gc[0:328, 0:64], gc[320:648, 0:64]], axis=1)
+        g[n, 328:USED] = jnp.concatenate([gc[160 * m : 160 * m + 168, 64:96] for m in range(4)], axis=1)
+        g[n, USED:ROWS] = jnp.zeros((ROWS - USED, 128), F32)
+
+    def core_reduce(bufs):
+        other = pl.multiple_of((1 - at["k"]) * 256, 256)
+        return send(bufs[0].at[:, pl.ds(other, 256)], bufs[1], shifted(at, k=1))
+
+    def x_reduce(bufs):
+        g, gr, h, hb, hr = bufs[:5]
+        sends = []
+        for by in (2, 1, 3, 0):
+            start = (at["x"] + by) % 4 * 64
+            value = (
+                g[:, pl.ds(pl.multiple_of(at["k"] * 256 + start, 64), 64)]
+                + gr[:, pl.ds(pl.multiple_of(start, 64), 64)]
+            )
+            if by == 0:
+                h[...] = value
+            else:
+                hb[by - 1] = value.astype(BF16)
+                sends.append(send(hb.at[by - 1], hr.at[by - 1], shifted(at, x=by)))
+        return sends
+
+    def z_reduce(bufs):
+        h, hr, zs, zr = bufs[2], bufs[4], bufs[5], bufs[6]
+        h[...] = h[...] + hr[0].astype(F32) + hr[1].astype(F32) + hr[2].astype(F32)
+        sends = []
+        for by in (3, 1, 2):
+            zs[by - 1] = h[:, pl.ds(pl.multiple_of((at["zl"] + by) % 4 * 16, 16), 16)]
+            sends.append(send(zs.at[by - 1], zr.at[by - 1], shifted(at, zl=by)))
+        return sends
+
+    def yz_gather(bufs, base):
+        h, zr, sb = bufs[2], bufs[6], bufs[7]
+        value = h[:, pl.ds(pl.multiple_of(at["zl"] * 16, 16), 16)] + zr[0] + zr[1] + zr[2]
+        sb[...] = (value * (1.0 / math.sqrt(40960))).astype(BF16)
+        piece = pl.multiple_of(at["k"] * 256 + at["x"] * 64 + at["zl"] * 16, 16)
+        sends = []
+        for n in range(2):
+            slot = SLOTS[base + n]
+            for dz in (3, 2, 1, 0):
+                if slot == 0 and dz == 0:
+                    ag[0, pl.ds(piece, 16)] = sb[0]
+                else:
+                    dst = ag.at[base + n, pl.ds(piece, 16)]
+                    sends.append(send(sb.at[n], dst, shifted(at, y=-slot, zl=dz)))
+        return sends
+
+    def x_gather(base):
+        start = pl.multiple_of(at["k"] * 256 + at["x"] * 64, 64)
+        ref = ag.at[pl.ds(base, 2), pl.ds(start, 64)]
+        return [send(ref, ref, shifted(at, x=by)) for by in (2, 1, 3)]
+
+    def core_gather(base):
+        ref = ag.at[pl.ds(base, 2), pl.ds(pl.multiple_of(at["k"] * 256, 256), 256)]
+        return send(ref, ref, shifted(at, k=1))
+
+    def unpack(place):
+        value = ag[place].astype(F32)
+        low, high = value[:328], value[328:USED]
+        left = jnp.concatenate([low[:, :64], low[8:, 64:]], axis=0)
+        right = jnp.concatenate(
+            [high[:, :32], high[8:, 32:64], high[8:, 64:96], high[8:, 96:]], axis=0
+        )
+        piece = jnp.concatenate([left, right], axis=1).astype(BF16)
+        return jnp.dot(piece, perm[SLOTS[place]], preferred_element_type=F32)
+
     for t in range(2):
         dsend[t : t + 1] = jnp.sum(p[t] * sx[t], axis=0, keepdims=True)
     dys = [send(dsend, dry.at[by - 1], shifted(at, y=by)) for by in (2, 1, 3)]
+    weigh(SLOTS[0], chain_a[0], 0)
+    weigh(SLOTS[1], chain_a[0], 1)
+    a = core_reduce(chain_a)
+    weigh(SLOTS[2], chain_b[0], 0)
+    weigh(SLOTS[3], chain_b[0], 1)
+    b = core_reduce(chain_b)
+    arrived([a])
+    a = x_reduce(chain_a)
+    arrived(dys)
+    dmid[...] = dsend[...] + dry[0] + dry[1] + dry[2]
+    dzs = [send(dmid, drz.at[by - 1], shifted(at, zh=by)) for by in (2, 1, 3)]
+    arrived([b])
+    b = x_reduce(chain_b)
     arrived(a)
     a = z_reduce(chain_a)
     arrived(b)
     b = z_reduce(chain_b)
-    arrived(dys)
-    dmid[...] = dsend[...] + dry[0] + dry[1] + dry[2]
-    dzs = [send(dmid, drz.at[by - 1], shifted(at, zh=by)) for by in (2, 1, 3)]
     arrived(a)
     a = yz_gather(chain_a, 0)
     arrived(b)
@@ -415,6 +413,8 @@
     f = jnp.transpose(features, (1, 0, 2, 3)).reshape(frames * chans, rows * cols)
     d = jnp.transpose(cotangent, (1, 0, 2, 3)).reshape(frames * chans, rows * cols)
     vmem = pl.BlockSpec(memory_space=pltpu.VMEM)
+    hbm = pl.BlockSpec(memory_space=pl.ANY)
+    w = jnp.transpose(conv_weight, (1, 0, 2)).reshape(27 * chans, TOTAL)
     sums = pltpu.VMEM((2, LANES), F32)
     sums3 = pltpu.VMEM((3, 2, LANES), F32)
     cells = pltpu.VMEM((3, 48, LANES), BF16)
@@ -425,11 +425,12 @@
             jax.ShapeDtypeStruct((648, TOTAL), BF16),
             jax.ShapeDtypeStruct((48, LANES), BF16),
         ),
-        in_specs=[vmem, vmem, pl.BlockSpec(memory_space=pl.ANY), vmem, vmem],
+        in_specs=[vmem, vmem, hbm, hbm, hbm],
         out_specs=(vmem, vmem),
         scratch_shapes=[
-            pltpu.VMEM((CH, 27, TOTAL), BF16),
-            pltpu.VMEM((3, CH * 32, 128), F32),
+            pltpu.VMEM((27 * CH, TOTAL), BF16),
+            pltpu.VMEM((TOTAL,), F32),
+            pltpu.VMEM((TOTAL,), F32),
             pltpu.VMEM((3, TOTAL, 9 * CH), F32),
             pltpu.VMEM((3, 288, 9 * CH), BF16),
             pltpu.VMEM((4, 288, 9 * CH), BF16),
@@ -459,14 +460,14 @@
             pltpu.VMEM((4, ROWS, 128), BF16),
             chain_buffers(),
             chain_buffers(),
-            pltpu.SemaphoreType.DMA,
+            pltpu.SemaphoreType.DMA((3,)),
             pltpu.SemaphoreType.DMA((COPIES,)),
             pltpu.SemaphoreType.DMA((COPIES,)),
         ],
         compiler_params=pltpu.CompilerParams(
             collective_id=0, has_side_effects=True, vmem_limit_bytes=40 << 20
         ),
-    )(f, d, conv_weight, norm_gain.reshape(1, TOTAL), norm_bias.reshape(1, TOTAL))
+    )(f, d, w, norm_gain, norm_bias)
     result = jnp.transpose(out.reshape(frames, chans, rows, cols), (1, 0, 2, 3))
     weight_grad = jnp.transpose(grads.reshape(27, chans, TOTAL), (1, 0, 2)).astype(F32)
     return result, weight_grad

time: 70.9 us -> 67.4 us (0.951)
  Pallas kernels: 64.7 us -> 62 us
  local copies, waits for them, and re-layouts: 4.25 us -> 3.5 us
    pallas_call x1, Pallas kernels: 64.7 us -> 62 us  [on_device(): pl.pallas_call(kernel, name='unit_backward', out_shape=(jax.ShapeDtypeStr...]
    unnamed x9 -> x6, local copies, waits for them, and re-layouts: 3.14 us -> 0.55 us
    transpose x1, local copies, waits for them, and re-layouts: 0.04 us -> 0.98 us  [on_device(): jnp.transpose(features, (1, 0, 2, 3)).reshape(frames * chans, rows * cols)]
    transpose x1, local copies, waits for them, and re-layouts: 0.04 us -> 0.93 us  [on_device(): jnp.transpose(cotangent, (1, 0, 2, 3)).reshape(frames * chans, rows * cols)]
where the time goes in v6:
time: 67.4 us; the launch traced here: 67.2 us
  Pallas kernels  62 us (92%)
  local copies, waits for them, and re-layouts  3.5 us (5%)
  other arithmetic  1.01 us (1%)
  between operations  0.69 us (1%)
    pallas_call x1, Pallas kernels, on_device(): pl.pallas_call(kernel, name='unit_backward', out_shape=(jax.ShapeDtypeStr...  62 us

profile of v6, /device:TPU:1, one launch (start us, length us, event | category | flops | bytes accessed | tf_op | source)
XLA Modules:
  0.0 67.2 jit_solution(14945253096432371883)
XLA Ops:
  0.6 0.0 copy-start
  0.6 1.0 %copy.7 = bf16[2,24,4,160]{3,2,1,0:T(4,128)(2,1)S(1)} copy(bf16[2,24,4,160]{3,2,0,1:T(4,128)(2,1)} %bitcast.14) | data formatting | bytes 122880 | tf_op jit(solution)/shard_map/transpose | solution.py:413
  1.6 0.1 reshape.19.f_ref
  1.8 0.9 %copy.8 = bf16[2,24,4,160]{3,2,1,0:T(4,128)(2,1)S(1)} copy(bf16[2,24,4,160]{3,2,0,1:T(4,128)(2,1)} %bitcast.15) | data formatting | bytes 122880 | tf_op jit(solution)/shard_map/transpose | solution.py:414
  2.7 0.0 copy-start.1
  2.7 0.0 copy-start.2
  2.7 0.1 reshape.20.d_ref
  2.8 0.0 copy-done
  2.8 0.5 copy-done.1
  3.4 0.0 copy-done.2
  3.4 62.0 %unit_backward.1 = (bf16[648,384]{1,0:T(8,128)(2,1)S(1)}, bf16[48,640]{1,0:T(8,128)(2,1)S(1)}) custom-call(bf16[48,640]{1,0:T(8,128)(2,1)S(1)} %reshape.19.f_ref, bf16[48,640]{1,0:T(8,128)(2,1)S(1)} %reshape.20.d_ref, bf16[648,384]{1,0:T(8,128)(2,1)S(1)} %bitcast.12, f32[384]{0:T(512)S(1)} %copy-done.1, f32[384]{0:T(512)S(1)} %copy-done.2), custom_call_target="tpu_custom_call" | custom-call | tf_op jit(solution)/shard_map/unit_backward/pallas_call | solution.py:421
  65.4 1.0 %convert_bitcast_fusion = f32[24,27,384]{2,0,1:T(8,128)} fusion(bf16[27,24,384]{2,1,0:T(8,128)(2,1)S(1)} %bitcast.13), kind=kLoop, calls=%fused_computation | loop fusion | flops 248832 | bytes 1492992 | tf_op jit(solution)/shard_map/convert_element_type | solution.py:472
  66.4 0.1 reshape.22
  66.5 0.7 %copy.11 = bf16[2,24,4,160]{3,2,0,1:T(4,128)(2,1)} copy(bf16[2,24,4,160]{3,2,1,0:T(4,128)(2,1)S(1)} %reshape.22) | data formatting | bytes 122880 | tf_op jit(solution)/shard_map/reshape | solution.py:471
Async XLA Ops:
  0.6 2.2 %copy-start = (bf16[24,27,384]{2,0,1:T(8,128)(2,1)S(1)}, bf16[24,27,384]{2,0,1:T(8,128)(2,1)}, u32[]{:S(2)}) copy-start(bf16[24,27,384]{2,0,1:T(8,128)(2,1)} %param.7) | copy-start | bytes 1492996
  2.7 0.7 %copy-start.1 = (f32[384]{0:T(512)S(1)}, f32[384]{0:T(512)}, u32[]{:S(2)}) copy-start(f32[384]{0:T(512)} %gain_hbm.1) | copy-start | bytes 4612
  2.7 0.7 %copy-start.2 = (f32[384]{0:T(512)S(1)}, f32[384]{0:T(512)}, u32[]{:S(2)}) copy-start(f32[384]{0:T(512)} %bias_hbm.1) | copy-start | bytes 4612

commit v7 on v6

--- a/solution.py
+++ b/solution.py
@@ -46,10 +46,11 @@
 
 
 def kernel(
-    f_ref, d_ref, raw_hbm, gain_hbm, bias_hbm, og_ref, od_ref,
+    fd_ref, raw_hbm, gain_hbm, bias_hbm, og_ref, od_ref,
     raw, gain_ref, bias_ref, tall, slabs, wall, gb_ref, dall, dnall, edall, fall, s9, p, q, qb, rz, act, sx, inv,
-    sown, smid, sry, srz, dsend, dmid, dry, drz, gc, perm, ag, chain_a, chain_b, lsem, ssem, rsem,
+    sown, smid, sry, srz, dsend, dmid, dry, drz, gc, perm, wgrad, ag, chain_a, chain_b, lsem, ssem, rsem,
 ):
+    f_ref, d_ref = fd_ref.at[0:48], fd_ref.at[48:96]
     at = coords()
     count = [0]
     started = []
@@ -90,33 +91,6 @@
     squares = squares * squares
     for t in range(2):
         sown[t : t + 1] = jnp.sum(squares[CH * t : CH * t + CH], axis=0, keepdims=True)
-    loads[0].wait()
-    loads[1].wait()
-    pair = [ref[...].reshape(1, TOTAL) for ref in (gain_ref, bias_ref)]
-    both = jnp.concatenate(pair + [jnp.zeros((6, TOTAL), F32)], axis=0)
-    gb_ref[...] = both.T
-
-    loads[2].wait()
-    for kt in range(3):
-        tall[kt] = raw[216 * kt : 216 * kt + 216].astype(F32).T
-
-    def slab(by):
-        y = (at["y"] + by) % 4
-        groups = [
-            tall[kt, pl.ds(pl.multiple_of(96 * zh + y * CH, 8), CH)] for kt in range(3) for zh in range(4)
-        ]
-        return jnp.concatenate(groups, axis=0).astype(BF16)
-
-    wall[0] = slab(0)
-    for by in (1, 2, 3):
-        slabs[by - 1] = slab(by)
-    r = lax.broadcasted_iota(jnp.int32, (96, TOTAL), 0)
-    lane = lax.broadcasted_iota(jnp.int32, (96, TOTAL), 1)
-    group = (r >= 24).astype(jnp.int32) + (r >= 48).astype(jnp.int32) + (r >= 72).astype(jnp.int32)
-    for s in range(4):
-        target = r + 72 * group + CH * ((at["y"] + s) % 4)
-        perm[s] = jnp.where(lane == target, 1.0, 0.0).astype(BF16)
-
     pl.semaphore_wait(barrier, len(greeted))
 
     row = at["zl"] * 2 + at["k"]
@@ -138,8 +112,22 @@
         [send(f_ref.at[rows], fall.at[at["zh"], rows], shifted(at, zh=by)) for by in (1, 3)] for rows in STEPS
     ]
     sys = [send(sown, sry.at[by - 1], shifted(at, y=by)) for by in (2, 1, 3)]
-    dy = {by: [send(d_ref, dall.at[by - 1], shifted(at, y=by))] for by in (2, 1, 3)}
-
+    dy = {by: [send(d_ref, dall.at[by - 1], shifted(at, y=by))] for by in (1, 3, 2)}
+
+    loads[2].wait()
+    for kt in range(3):
+        tall[kt] = raw[216 * kt : 216 * kt + 216].astype(F32).T
+
+    def slab(by):
+        y = (at["y"] + by) % 4
+        groups = [
+            tall[kt, pl.ds(pl.multiple_of(96 * zh + y * CH, 8), CH)] for kt in range(3) for zh in range(4)
+        ]
+        return jnp.concatenate(groups, axis=0).astype(BF16)
+
+    wall[0] = slab(0)
+    for by in (1, 2, 3):
+        slabs[by - 1] = slab(by)
     half = pl.multiple_of(at["k"] * 144, 16)
     ws = [
         send(slabs.at[by - 1, pl.ds(half, 144)], wall.at[by, pl.ds(half, 144)], shifted(at, y=by))
@@ -147,11 +135,11 @@
     ]
 
     arrived([frame])
-    for by in (2, 1, 3):
+    for by in (1, 3, 2):
         dy[by].append(send(dnall.at[0], dnall.at[by], shifted(at, y=by)))
     for copy, _, comes in halo:
         pl.when(comes)(copy.wait_recv)
-    for by in (2, 1, 3):
+    for by in (1, 3, 2):
         dy[by].append(send(edall.at[0], edall.at[by], shifted(at, y=by)))
     column = lax.broadcasted_iota(jnp.int32, (CH, LANES), 1) % 160
     left_end, right_end = column == 0, column == 159
@@ -181,6 +169,17 @@
                 pieces.append(jnp.where(left_end, 0.0, pltpu.roll(one, 1, 1)))
             s9[slot, tp] = jnp.concatenate(pieces, axis=0).astype(BF16)
 
+    def dgrad(slot):
+        for tp, (low, high) in enumerate(((192, 288), (96, 288), (0, 192), (0, 96))):
+            part = jnp.dot(wall[slot, low:high], s9[slot, tp], preferred_element_type=F32)
+            for n in range((high - low) // 96):
+                t = n if high - low > 96 else tp // 3
+                piece = part[96 * n : 96 * n + 96]
+                if slot == 0 and (tp == 0 or (tp == 1 and t == 1)):
+                    p[t] = piece
+                else:
+                    p[t] += piece
+
     side = 1 + 2 * at["k"]
     source = (at["zh"] + side) % 4
     away = {"tm": at["x"], "height": row, "chan": (at["zh"] + 4 - side) % 4 * 4 + at["y"]}
@@ -197,42 +196,33 @@
     far_step(0)
     build(0)
     far_step(1)
+    dgrad(0)
     far_step(2)
     arrived(ws)
     ref = wall.at[pl.ds(1, 3), pl.ds(half, 144)]
     wx = send(ref, ref, shifted(at, k=1))
     arrived(szs)
     szf = send(smid.at[1], srz, shifted(at, zh=1))
-    for by in (1, 3, 2):
-        arrived(dy[by])
-        build(by)
-
+    loads[0].wait()
+    loads[1].wait()
+    pair = [ref[...].reshape(1, TOTAL) for ref in (gain_ref, bias_ref)]
+    both = jnp.concatenate(pair + [jnp.zeros((6, TOTAL), F32)], axis=0)
+    gb_ref[...] = both.T
+
+    r = lax.broadcasted_iota(jnp.int32, (96, TOTAL), 0)
+    lane = lax.broadcasted_iota(jnp.int32, (96, TOTAL), 1)
+    group = (r >= 24).astype(jnp.int32) + (r >= 48).astype(jnp.int32) + (r >= 72).astype(jnp.int32)
+    for s in range(4):
+        target = r + 72 * group + CH * ((at["y"] + s) % 4)
+        perm[s] = jnp.where(lane == target, 1.0, 0.0).astype(BF16)
+
+    arrived(dy[1])
+    build(1)
     arrived([wx])
-    for tp, (low, high) in enumerate(((192, 288), (96, 288), (0, 192), (0, 96))):
-        total = None
-        for slot in range(4):
-            part = jnp.dot(wall[slot, low:high], s9[slot, tp], preferred_element_type=F32)
-            total = part if total is None else total + part
-        if tp == 0:
-            p[0] = total
-        elif tp == 1:
-            p[0] += total[:96]
-            p[1] = total[96:]
-        elif tp == 2:
-            p[0] += total[:96]
-            p[1] += total[96:]
-        else:
-            p[1] += total
-
-    zsends = []
-    for by in (2, 1, 3, 0):
-        start = pl.multiple_of((at["zh"] + by) % 4 * CH, 8)
-        value = jnp.concatenate([p[0, pl.ds(start, CH)], p[1, pl.ds(start, CH)]], axis=0)
-        if by == 0:
-            q[...] = value
-        else:
-            qb[by - 1] = value.astype(BF16)
-            zsends.append(send(qb.at[by - 1], rz.at[by - 1], shifted(at, zh=by)))
+    dgrad(1)
+    arrived(dy[3])
+    build(3)
+    dgrad(3)
     arrived([szf])
     total = smid[0] + smid[1] + smid[3] + srz[...]
     inv[...] = lax.rsqrt(total * (1.0 / TOTAL) + 1e-06)
@@ -338,12 +328,24 @@
         piece = jnp.concatenate([left, right], axis=1).astype(BF16)
         return jnp.dot(piece, perm[SLOTS[place]], preferred_element_type=F32)
 
+    weigh(SLOTS[0], chain_a[0], 0)
+    weigh(SLOTS[1], chain_a[0], 1)
+    a = core_reduce(chain_a)
+    arrived(dy[2])
+    build(2)
+    dgrad(2)
+    zsends = []
+    for by in (2, 1, 3, 0):
+        start = pl.multiple_of((at["zh"] + by) % 4 * CH, 8)
+        value = jnp.concatenate([p[0, pl.ds(start, CH)], p[1, pl.ds(start, CH)]], axis=0)
+        if by == 0:
+            q[...] = value
+        else:
+            qb[by - 1] = value.astype(BF16)
+            zsends.append(send(qb.at[by - 1], rz.at[by - 1], shifted(at, zh=by)))
     for t in range(2):
         dsend[t : t + 1] = jnp.sum(p[t] * sx[t], axis=0, keepdims=True)
     dys = [send(dsend, dry.at[by - 1], shifted(at, y=by)) for by in (2, 1, 3)]
-    weigh(SLOTS[0], chain_a[0], 0)
-    weigh(SLOTS[1], chain_a[0], 1)
-    a = core_reduce(chain_a)
     weigh(SLOTS[2], chain_b[0], 0)
     weigh(SLOTS[3], chain_b[0], 1)
     b = core_reduce(chain_b)
@@ -387,8 +389,10 @@
         outs.append(ct[rows] + back)
     od_ref[...] = jnp.concatenate(outs, axis=0).astype(BF16)
 
-    arrived([a, b])
-    og_ref[...] = (unpack(0) + unpack(1) + unpack(2) + unpack(3)).astype(BF16)
+    arrived([a])
+    wgrad[...] = unpack(0) + unpack(1)
+    arrived([b])
+    og_ref[...] = (wgrad[...] + unpack(2) + unpack(3)).astype(BF16)
     for copy in started:
         copy.wait_send()
     for copy, goes, _ in halo:
@@ -410,8 +414,8 @@
 
 def on_device(features, cotangent, conv_weight, norm_gain, norm_bias):
     chans, frames, rows, cols = features.shape
-    f = jnp.transpose(features, (1, 0, 2, 3)).reshape(frames * chans, rows * cols)
-    d = jnp.transpose(cotangent, (1, 0, 2, 3)).reshape(frames * chans, rows * cols)
+    fd = jnp.transpose(jnp.stack([features, cotangent]), (0, 2, 1, 3, 4))
+    fd = fd.reshape(2 * frames * chans, rows * cols)
     vmem = pl.BlockSpec(memory_space=pltpu.VMEM)
     hbm = pl.BlockSpec(memory_space=pl.ANY)
     w = jnp.transpose(conv_weight, (1, 0, 2)).reshape(27 * chans, TOTAL)
@@ -425,7 +429,7 @@
             jax.ShapeDtypeStruct((648, TOTAL), BF16),
             jax.ShapeDtypeStruct((48, LANES), BF16),
         ),
-        in_specs=[vmem, vmem, hbm, hbm, hbm],
+        in_specs=[vmem, hbm, hbm, hbm],
         out_specs=(vmem, vmem),
         scratch_shapes=[
             pltpu.VMEM((27 * CH, TOTAL), BF16),
@@ -457,6 +461,7 @@
             sums3,
             pltpu.VMEM((648, 96), F32),
             pltpu.VMEM((4, 96, TOTAL), BF16),
+            pltpu.VMEM((648, TOTAL), F32),
             pltpu.VMEM((4, ROWS, 128), BF16),
             chain_buffers(),
             chain_buffers(),
@@ -467,7 +472,7 @@
         compiler_params=pltpu.CompilerParams(
             collective_id=0, has_side_effects=True, vmem_limit_bytes=40 << 20
         ),
-    )(f, d, w, norm_gain, norm_bias)
+    )(fd, w, norm_gain, norm_bias)
     result = jnp.transpose(out.reshape(frames, chans, rows, cols), (1, 0, 2, 3))
     weight_grad = jnp.transpose(grads.reshape(27, chans, TOTAL), (1, 0, 2)).astype(F32)
     return result, weight_grad

time: 67.4 us -> 66.9 us (level)
  local copies, waits for them, and re-layouts: 3.5 us -> 1.53 us
  other arithmetic: 1.01 us -> 2.17 us
    transpose x2 -> x1, local copies, waits for them, and re-layouts: 1.91 us -> 0.07 us  [on_device(): fd = jnp.transpose(jnp.stack([features, cotangent]), (0, 2, 1, 3, 4))]
    transpose x0 -> x1, other arithmetic: none -> 1.15 us  [on_device(): fd = jnp.transpose(jnp.stack([features, cotangent]), (0, 2, 1, 3, 4))]
where the time goes in v7:
time: 66.9 us; the launch traced here: 66.8 us
  Pallas kernels  62.4 us (93%)
  other arithmetic  2.17 us (3%)
  local copies, waits for them, and re-layouts  1.53 us (2%)
  between operations  0.7 us (1%)
    pallas_call x1, Pallas kernels, on_device(): pl.pallas_call(kernel, name='unit_backward', out_shape=(jax.ShapeDtypeStr...  62.4 us

profile of v7, /device:TPU:1, one launch (start us, length us, event | category | flops | bytes accessed | tf_op | source)
XLA Modules:
  0.0 66.8 jit_solution(13124031657250993492)
XLA Ops:
  0.6 0.0 copy-start
  0.6 1.2 %maximum_bitcast_fusion = bf16[2,2,24,4,160]{4,3,1,2,0:T(4,128)(2,1)S(1)} fusion(bf16[1,24,2,4,160]{4,3,2,1,0:T(4,128)(2,1)} %bitcast.17, bf16[1,24,2,4,160]{4,3,2,1,0:T(4,128)(2,1)} %bitcast.18), kind=kLoop, calls=%fused_computation.1 | loop fusion | flops 61440 | bytes 245760 | tf_op jit(solution)/shard_map/transpose | solution.py:417
  1.8 0.1 copy.7
  1.9 0.0 copy-start.1
  1.9 0.0 copy-start.2
  1.9 0.2 reshape.16.fd_ref
  2.1 0.0 copy-done
  2.1 0.5 copy-done.1
  2.6 0.0 copy-done.2
  2.6 62.4 %unit_backward.1 = (bf16[648,384]{1,0:T(8,128)(2,1)S(1)}, bf16[48,640]{1,0:T(8,128)(2,1)S(1)}) custom-call(bf16[96,640]{1,0:T(8,128)(2,1)S(1)} %reshape.16.fd_ref, bf16[648,384]{1,0:T(8,128)(2,1)S(1)} %bitcast.14, f32[384]{0:T(512)S(1)} %copy-done.1, f32[384]{0:T(512)S(1)} %copy-done.2), custom_call_target="tpu_custom_call" | custom-call | tf_op jit(solution)/shard_map/unit_backward/pallas_call | solution.py:425
  65.0 1.0 %convert_bitcast_fusion = f32[24,27,384]{2,0,1:T(8,128)} fusion(bf16[27,24,384]{2,1,0:T(8,128)(2,1)S(1)} %bitcast.15), kind=kLoop, calls=%fused_computation | loop fusion | flops 248832 | bytes 1492992 | tf_op jit(solution)/shard_map/convert_element_type | solution.py:477
  66.0 0.1 reshape.18
  66.1 0.7 %copy.10 = bf16[2,24,4,160]{3,2,0,1:T(4,128)(2,1)} copy(bf16[2,24,4,160]{3,2,1,0:T(4,128)(2,1)S(1)} %reshape.18) | data formatting | bytes 122880 | tf_op jit(solution)/shard_map/reshape | solution.py:476
Async XLA Ops:
  0.6 1.4 %copy-start = (bf16[24,27,384]{2,0,1:T(8,128)(2,1)S(1)}, bf16[24,27,384]{2,0,1:T(8,128)(2,1)}, u32[]{:S(2)}) copy-start(bf16[24,27,384]{2,0,1:T(8,128)(2,1)} %param.7) | copy-start | bytes 1492996
  1.9 0.7 %copy-start.1 = (f32[384]{0:T(512)S(1)}, f32[384]{0:T(512)}, u32[]{:S(2)}) copy-start(f32[384]{0:T(512)} %gain_hbm.1) | copy-start | bytes 4612
  1.9 0.7 %copy-start.2 = (f32[384]{0:T(512)S(1)}, f32[384]{0:T(512)}, u32[]{:S(2)}) copy-start(f32[384]{0:T(512)} %bias_hbm.1) | copy-start | bytes 4612

commit v8 on v7

--- a/solution.py
+++ b/solution.py
@@ -128,12 +128,6 @@
     wall[0] = slab(0)
     for by in (1, 2, 3):
         slabs[by - 1] = slab(by)
-    half = pl.multiple_of(at["k"] * 144, 16)
-    ws = [
-        send(slabs.at[by - 1, pl.ds(half, 144)], wall.at[by, pl.ds(half, 144)], shifted(at, y=by))
-        for by in (2, 1, 3)
-    ]
-
     arrived([frame])
     for by in (1, 3, 2):
         dy[by].append(send(dnall.at[0], dnall.at[by], shifted(at, y=by)))
@@ -141,6 +135,13 @@
         pl.when(comes)(copy.wait_recv)
     for by in (1, 3, 2):
         dy[by].append(send(edall.at[0], edall.at[by], shifted(at, y=by)))
+    half = pl.multiple_of(at["k"] * 144, 16)
+    ws = [
+        send(slabs.at[by - 1, pl.ds(half, 144)], wall.at[by, pl.ds(half, 144)], shifted(at, y=by))
+        for by in (2, 1, 3)
+    ]
+
+
     column = lax.broadcasted_iota(jnp.int32, (CH, LANES), 1) % 160
     left_end, right_end = column == 0, column == 159
     next_on = jnp.where(at["x"] < 3, 1.0, 0.0).astype(F32)
@@ -198,9 +199,6 @@
     far_step(1)
     dgrad(0)
     far_step(2)
-    arrived(ws)
-    ref = wall.at[pl.ds(1, 3), pl.ds(half, 144)]
-    wx = send(ref, ref, shifted(at, k=1))
     arrived(szs)
     szf = send(smid.at[1], srz, shifted(at, zh=1))
     loads[0].wait()
@@ -218,11 +216,8 @@
 
     arrived(dy[1])
     build(1)
-    arrived([wx])
-    dgrad(1)
     arrived(dy[3])
     build(3)
-    dgrad(3)
     arrived([szf])
     total = smid[0] + smid[1] + smid[3] + srz[...]
     inv[...] = lax.rsqrt(total * (1.0 / TOTAL) + 1e-06)
@@ -333,7 +328,27 @@
     a = core_reduce(chain_a)
     arrived(dy[2])
     build(2)
+    arrived(ws)
+    ref = wall.at[pl.ds(1, 3), pl.ds(half, 144)]
+    wx = send(ref, ref, shifted(at, k=1))
+    weigh(SLOTS[2], chain_b[0], 0)
+    weigh(SLOTS[3], chain_b[0], 1)
+    b = core_reduce(chain_b)
+    arrived([a])
+    a = x_reduce(chain_a)
+    arrived([wx])
+    dgrad(1)
+    arrived([b])
+    b = x_reduce(chain_b)
+    dgrad(3)
     dgrad(2)
+    for t in range(2):
+        dsend[t : t + 1] = jnp.sum(p[t] * sx[t], axis=0, keepdims=True)
+    dys = [send(dsend, dry.at[by - 1], shifted(at, y=by)) for by in (2, 1, 3)]
+    arrived(a)
+    a = z_reduce(chain_a)
+    arrived(b)
+    b = z_reduce(chain_b)
     zsends = []
     for by in (2, 1, 3, 0):
         start = pl.multiple_of((at["zh"] + by) % 4 * CH, 8)
@@ -343,23 +358,9 @@
         else:
             qb[by - 1] = value.astype(BF16)
             zsends.append(send(qb.at[by - 1], rz.at[by - 1], shifted(at, zh=by)))
-    for t in range(2):
-        dsend[t : t + 1] = jnp.sum(p[t] * sx[t], axis=0, keepdims=True)
-    dys = [send(dsend, dry.at[by - 1], shifted(at, y=by)) for by in (2, 1, 3)]
-    weigh(SLOTS[2], chain_b[0], 0)
-    weigh(SLOTS[3], chain_b[0], 1)
-    b = core_reduce(chain_b)
-    arrived([a])
-    a = x_reduce(chain_a)
     arrived(dys)
     dmid[...] = dsend[...] + dry[0] + dry[1] + dry[2]
     dzs = [send(dmid, drz.at[by - 1], shifted(at, zh=by)) for by in (2, 1, 3)]
-    arrived([b])
-    b = x_reduce(chain_b)
-    arrived(a)
-    a = z_reduce(chain_a)
-    arrived(b)
-    b = z_reduce(chain_b)
     arrived(a)
     a = yz_gather(chain_a, 0)
     arrived(b)

time: 66.9 us -> 70.1 us (1.048)
  Pallas kernels: 62.4 us -> 65.6 us
    pallas_call x1, Pallas kernels: 62.4 us -> 65.6 us  [on_device(): pl.pallas_call(kernel, name='unit_backward', out_shape=(jax.ShapeDtypeStr...]
where the time goes in v8:
time: 70.1 us; the launch traced here: 70 us
  Pallas kernels  65.6 us (94%)
  other arithmetic  2.17 us (3%)
  local copies, waits for them, and re-layouts  1.53 us (2%)
    pallas_call x1, Pallas kernels, on_device(): pl.pallas_call(kernel, name='unit_backward', out_shape=(jax.ShapeDtypeStr...  65.6 us

profile of v8, /device:TPU:1, one launch (start us, length us, event | category | flops | bytes accessed | tf_op | source)
XLA Modules:
  0.0 70.0 jit_solution(9091399891987897248)
XLA Ops:
  0.6 0.0 copy-start
  0.6 1.2 %maximum_bitcast_fusion = bf16[2,2,24,4,160]{4,3,1,2,0:T(4,128)(2,1)S(1)} fusion(bf16[1,24,2,4,160]{4,3,2,1,0:T(4,128)(2,1)} %bitcast.17, bf16[1,24,2,4,160]{4,3,2,1,0:T(4,128)(2,1)} %bitcast.18), kind=kLoop, calls=%fused_computation.1 | loop fusion | flops 61440 | bytes 245760 | tf_op jit(solution)/shard_map/transpose | solution.py:418
  1.8 0.1 copy.7
  1.9 0.0 copy-start.1
  1.9 0.0 copy-start.2
  1.9 0.2 reshape.16.fd_ref
  2.1 0.0 copy-done
  2.1 0.5 copy-done.1
  2.6 0.0 copy-done.2
  2.6 65.6 %unit_backward.1 = (bf16[648,384]{1,0:T(8,128)(2,1)S(1)}, bf16[48,640]{1,0:T(8,128)(2,1)S(1)}) custom-call(bf16[96,640]{1,0:T(8,128)(2,1)S(1)} %reshape.16.fd_ref, bf16[648,384]{1,0:T(8,128)(2,1)S(1)} %bitcast.14, f32[384]{0:T(512)S(1)} %copy-done.1, f32[384]{0:T(512)S(1)} %copy-done.2), custom_call_target="tpu_custom_call" | custom-call | tf_op jit(solution)/shard_map/unit_backward/pallas_call | solution.py:426
  68.2 1.0 %convert_bitcast_fusion = f32[24,27,384]{2,0,1:T(8,128)} fusion(bf16[27,24,384]{2,1,0:T(8,128)(2,1)S(1)} %bitcast.15), kind=kLoop, calls=%fused_computation | loop fusion | flops 248832 | bytes 1492992 | tf_op jit(solution)/shard_map/convert_element_type | solution.py:478
  69.2 0.1 reshape.18
  69.3 0.7 copy.10
Async XLA Ops:
  0.6 1.4 %copy-start = (bf16[24,27,384]{2,0,1:T(8,128)(2,1)S(1)}, bf16[24,27,384]{2,0,1:T(8,128)(2,1)}, u32[]{:S(2)}) copy-start(bf16[24,27,384]{2,0,1:T(8,128)(2,1)} %param.7) | copy-start | bytes 1492996
  1.9 0.7 copy-start.1
  1.9 0.7 copy-start.2

commit v9 on v7

--- a/solution.py
+++ b/solution.py
@@ -334,23 +334,27 @@
     arrived(dy[2])
     build(2)
     dgrad(2)
-    zsends = []
-    for by in (2, 1, 3, 0):
+    def grad_part(by):
         start = pl.multiple_of((at["zh"] + by) % 4 * CH, 8)
-        value = jnp.concatenate([p[0, pl.ds(start, CH)], p[1, pl.ds(start, CH)]], axis=0)
-        if by == 0:
-            q[...] = value
-        else:
-            qb[by - 1] = value.astype(BF16)
-            zsends.append(send(qb.at[by - 1], rz.at[by - 1], shifted(at, zh=by)))
+        return jnp.concatenate([p[0, pl.ds(start, CH)], p[1, pl.ds(start, CH)]], axis=0)
+
+    along = {"tm": at["x"], "height": row, "chan": (at["zh"] + side) % 4 * 4 + at["y"]}
+    qb[0] = grad_part(2).astype(BF16)
+    z_far = send(qb.at[0], rz.at[0], along)
+    qb[1] = grad_part(4 - side).astype(BF16)
+    z_near = send(qb.at[1], rz.at[1], away)
+    q[...] = grad_part(0)
+    arrived([a])
+    a = x_reduce(chain_a)
     for t in range(2):
         dsend[t : t + 1] = jnp.sum(p[t] * sx[t], axis=0, keepdims=True)
     dys = [send(dsend, dry.at[by - 1], shifted(at, y=by)) for by in (2, 1, 3)]
     weigh(SLOTS[2], chain_b[0], 0)
     weigh(SLOTS[3], chain_b[0], 1)
     b = core_reduce(chain_b)
-    arrived([a])
-    a = x_reduce(chain_a)
+    arrived([z_far])
+    qb[2] = (grad_part(side) + rz[0].astype(F32)).astype(BF16)
+    z_sum = send(qb.at[2], rz.at[2], along)
     arrived(dys)
     dmid[...] = dsend[...] + dry[0] + dry[1] + dry[2]
     dzs = [send(dmid, drz.at[by - 1], shifted(at, zh=by)) for by in (2, 1, 3)]
@@ -373,8 +377,8 @@
     arrived(b)
     b = core_gather(2)
 
-    arrived(zsends + dzs)
-    grad = q[...] + rz[0].astype(F32) + rz[1].astype(F32) + rz[2].astype(F32)
+    arrived([z_near, z_sum] + dzs)
+    grad = q[...] + rz[1].astype(F32) + rz[2].astype(F32)
     dots = dmid[...] + drz[0] + drz[1] + drz[2]
     mine_x = f_ref[...].astype(F32)
     ct = d_ref[...].astype(F32)

time: 66.9 us -> 66.2 us (0.990)
  Pallas kernels: 62.4 us -> 61.7 us
    pallas_call x1, Pallas kernels: 62.4 us -> 61.7 us  [on_device(): pl.pallas_call(kernel, name='unit_backward', out_shape=(jax.ShapeDtypeStr...]
where the time goes in v9:
time: 66.2 us; the launch traced here: 66.1 us
  Pallas kernels  61.7 us (93%)
  other arithmetic  2.17 us (3%)
  local copies, waits for them, and re-layouts  1.53 us (2%)
  between operations  0.7 us (1%)
    pallas_call x1, Pallas kernels, on_device(): pl.pallas_call(kernel, name='unit_backward', out_shape=(jax.ShapeDtypeStr...  61.7 us

profile of v9, /device:TPU:1, one launch (start us, length us, event | category | flops | bytes accessed | tf_op | source)
XLA Modules:
  0.0 66.1 jit_solution(18172995604424037582)
XLA Ops:
  0.6 0.0 copy-start
  0.6 1.2 %maximum_bitcast_fusion = bf16[2,2,24,4,160]{4,3,1,2,0:T(4,128)(2,1)S(1)} fusion(bf16[1,24,2,4,160]{4,3,2,1,0:T(4,128)(2,1)} %bitcast.17, bf16[1,24,2,4,160]{4,3,2,1,0:T(4,128)(2,1)} %bitcast.18), kind=kLoop, calls=%fused_computation.1 | loop fusion | flops 61440 | bytes 245760 | tf_op jit(solution)/shard_map/transpose | solution.py:421
  1.8 0.1 copy.7
  1.9 0.0 copy-start.1
  1.9 0.0 copy-start.2
  1.9 0.2 reshape.16.fd_ref
  2.1 0.0 copy-done
  2.1 0.5 copy-done.1
  2.6 0.0 copy-done.2
  2.6 61.7 %unit_backward.1 = (bf16[648,384]{1,0:T(8,128)(2,1)S(1)}, bf16[48,640]{1,0:T(8,128)(2,1)S(1)}) custom-call(bf16[96,640]{1,0:T(8,128)(2,1)S(1)} %reshape.16.fd_ref, bf16[648,384]{1,0:T(8,128)(2,1)S(1)} %bitcast.14, f32[384]{0:T(512)S(1)} %copy-done.1, f32[384]{0:T(512)S(1)} %copy-done.2), custom_call_target="tpu_custom_call" | custom-call | tf_op jit(solution)/shard_map/unit_backward/pallas_call | solution.py:429
  64.3 1.0 %convert_bitcast_fusion = f32[24,27,384]{2,0,1:T(8,128)} fusion(bf16[27,24,384]{2,1,0:T(8,128)(2,1)S(1)} %bitcast.15), kind=kLoop, calls=%fused_computation | loop fusion | flops 248832 | bytes 1492992 | tf_op jit(solution)/shard_map/convert_element_type | solution.py:481
  65.3 0.1 reshape.18
  65.4 0.7 %copy.10 = bf16[2,24,4,160]{3,2,0,1:T(4,128)(2,1)} copy(bf16[2,24,4,160]{3,2,1,0:T(4,128)(2,1)S(1)} %reshape.18) | data formatting | bytes 122880 | tf_op jit(solution)/shard_map/reshape | solution.py:480
Async XLA Ops:
  0.6 1.4 %copy-start = (bf16[24,27,384]{2,0,1:T(8,128)(2,1)S(1)}, bf16[24,27,384]{2,0,1:T(8,128)(2,1)}, u32[]{:S(2)}) copy-start(bf16[24,27,384]{2,0,1:T(8,128)(2,1)} %param.7) | copy-start | bytes 1492996
  1.9 0.7 %copy-start.1 = (f32[384]{0:T(512)S(1)}, f32[384]{0:T(512)}, u32[]{:S(2)}) copy-start(f32[384]{0:T(512)} %gain_hbm.1) | copy-start | bytes 4612
  1.9 0.7 %copy-start.2 = (f32[384]{0:T(512)S(1)}, f32[384]{0:T(512)}, u32[]{:S(2)}) copy-start(f32[384]{0:T(512)} %bias_hbm.1) | copy-start | bytes 4612

commit v10 on v9

--- a/solution.py
+++ b/solution.py
@@ -352,20 +352,20 @@
     weigh(SLOTS[2], chain_b[0], 0)
     weigh(SLOTS[3], chain_b[0], 1)
     b = core_reduce(chain_b)
-    arrived([z_far])
-    qb[2] = (grad_part(side) + rz[0].astype(F32)).astype(BF16)
-    z_sum = send(qb.at[2], rz.at[2], along)
+    arrived(a)
+    a = z_reduce(chain_a)
     arrived(dys)
     dmid[...] = dsend[...] + dry[0] + dry[1] + dry[2]
     dzs = [send(dmid, drz.at[by - 1], shifted(at, zh=by)) for by in (2, 1, 3)]
     arrived([b])
     b = x_reduce(chain_b)
+    arrived([z_far])
+    qb[2] = (grad_part(side) + rz[0].astype(F32)).astype(BF16)
+    z_sum = send(qb.at[2], rz.at[2], along)
     arrived(a)
-    a = z_reduce(chain_a)
+    a = yz_gather(chain_a, 0)
     arrived(b)
     b = z_reduce(chain_b)
-    arrived(a)
-    a = yz_gather(chain_a, 0)
     arrived(b)
     b = yz_gather(chain_b, 2)
     arrived(a)
@@ -374,8 +374,6 @@
     b = x_gather(2)
     arrived(a)
     a = core_gather(0)
-    arrived(b)
-    b = core_gather(2)
 
     arrived([z_near, z_sum] + dzs)
     grad = q[...] + rz[1].astype(F32) + rz[2].astype(F32)
@@ -393,6 +391,8 @@
         outs.append(ct[rows] + back)
     od_ref[...] = jnp.concatenate(outs, axis=0).astype(BF16)
 
+    arrived(b)
+    b = core_gather(2)
     arrived([a])
     wgrad[...] = unpack(0) + unpack(1)
     arrived([b])

time: 66.2 us -> 65.9 us (level)
  no operation moved by 1% of the time
where the time goes in v10:
time: 65.9 us; the launch traced here: 65.8 us
  Pallas kernels  61.4 us (93%)
  other arithmetic  2.17 us (3%)
  local copies, waits for them, and re-layouts  1.53 us (2%)
  between operations  0.7 us (1%)
    pallas_call x1, Pallas kernels, on_device(): pl.pallas_call(kernel, name='unit_backward', out_shape=(jax.ShapeDtypeStr...  61.4 us

profile of v10, /device:TPU:1, one launch (start us, length us, event | category | flops | bytes accessed | tf_op | source)
XLA Modules:
  0.0 65.8 jit_solution(8371619076215007597)
XLA Ops:
  0.6 0.0 copy-start
  0.6 1.2 %maximum_bitcast_fusion = bf16[2,2,24,4,160]{4,3,1,2,0:T(4,128)(2,1)S(1)} fusion(bf16[1,24,2,4,160]{4,3,2,1,0:T(4,128)(2,1)} %bitcast.17, bf16[1,24,2,4,160]{4,3,2,1,0:T(4,128)(2,1)} %bitcast.18), kind=kLoop, calls=%fused_computation.1 | loop fusion | flops 61440 | bytes 245760 | tf_op jit(solution)/shard_map/transpose | solution.py:421
  1.8 0.1 copy.7
  1.9 0.0 copy-start.1
  1.9 0.0 copy-start.2
  1.9 0.2 reshape.16.fd_ref
  2.1 0.0 copy-done
  2.1 0.5 copy-done.1
  2.6 0.0 copy-done.2
  2.6 61.4 %unit_backward.1 = (bf16[648,384]{1,0:T(8,128)(2,1)S(1)}, bf16[48,640]{1,0:T(8,128)(2,1)S(1)}) custom-call(bf16[96,640]{1,0:T(8,128)(2,1)S(1)} %reshape.16.fd_ref, bf16[648,384]{1,0:T(8,128)(2,1)S(1)} %bitcast.14, f32[384]{0:T(512)S(1)} %copy-done.1, f32[384]{0:T(512)S(1)} %copy-done.2), custom_call_target="tpu_custom_call" | custom-call | tf_op jit(solution)/shard_map/unit_backward/pallas_call | solution.py:429
  64.0 1.0 %convert_bitcast_fusion = f32[24,27,384]{2,0,1:T(8,128)} fusion(bf16[27,24,384]{2,1,0:T(8,128)(2,1)S(1)} %bitcast.15), kind=kLoop, calls=%fused_computation | loop fusion | flops 248832 | bytes 1492992 | tf_op jit(solution)/shard_map/convert_element_type | solution.py:481
  65.0 0.1 reshape.18
  65.1 0.7 %copy.10 = bf16[2,24,4,160]{3,2,0,1:T(4,128)(2,1)} copy(bf16[2,24,4,160]{3,2,1,0:T(4,128)(2,1)S(1)} %reshape.18) | data formatting | bytes 122880 | tf_op jit(solution)/shard_map/reshape | solution.py:480
Async XLA Ops:
  0.6 1.4 %copy-start = (bf16[24,27,384]{2,0,1:T(8,128)(2,1)S(1)}, bf16[24,27,384]{2,0,1:T(8,128)(2,1)}, u32[]{:S(2)}) copy-start(bf16[24,27,384]{2,0,1:T(8,128)(2,1)} %param.7) | copy-start | bytes 1492996
  1.9 0.7 %copy-start.1 = (f32[384]{0:T(512)S(1)}, f32[384]{0:T(512)}, u32[]{:S(2)}) copy-start(f32[384]{0:T(512)} %gain_hbm.1) | copy-start | bytes 4612
  1.9 0.7 %copy-start.2 = (f32[384]{0:T(512)S(1)}, f32[384]{0:T(512)}, u32[]{:S(2)}) copy-start(f32[384]{0:T(512)} %bias_hbm.1) | copy-start | bytes 4612

commit v11 on v10

--- a/solution.py
+++ b/solution.py
@@ -47,7 +47,7 @@
 
 def kernel(
     fd_ref, raw_hbm, gain_hbm, bias_hbm, og_ref, od_ref,
-    raw, gain_ref, bias_ref, tall, slabs, wall, gb_ref, dall, dnall, edall, fall, s9, p, q, qb, rz, act, sx, inv,
+    raw, gain_ref, bias_ref, tall, slabs, wall, gb_ref, dall, dnall, edall, joint, fall, s9, p, q, qb, rz, act, sx, inv,
     sown, smid, sry, srz, dsend, dmid, dry, drz, gc, perm, wgrad, ag, chain_a, chain_b, lsem, ssem, rsem,
 ):
     f_ref, d_ref = fd_ref.at[0:48], fd_ref.at[48:96]
@@ -76,7 +76,7 @@
     ]
     for copy in loads:
         copy.start()
-    edall[0] = jnp.zeros((4, 48, 256), BF16)
+    edall[...] = jnp.zeros((4, 48, 256), BF16)
     barrier = pltpu.get_barrier_semaphore()
     greeted = [shifted(at, zh=1), shifted(at, zh=3)]
     greeted += [neighbour(at, -dx, -dh) for dx, dh in HALO]
@@ -101,7 +101,7 @@
         i = count[0]
         count[0] += 1
         copy = pltpu.make_async_remote_copy(
-            src_ref=d_ref.at[:, pl.ds(384 if dh == 1 else 0, 256)], dst_ref=edall.at[0, n],
+            src_ref=d_ref.at[:, pl.ds(384 if dh == 1 else 0, 256)], dst_ref=edall.at[n],
             send_sem=ssem.at[i], recv_sem=rsem.at[i],
             device_id=neighbour(at, dx, dh), device_id_type=MESH,
         )
@@ -139,8 +139,12 @@
         dy[by].append(send(dnall.at[0], dnall.at[by], shifted(at, y=by)))
     for copy, _, comes in halo:
         pl.when(comes)(copy.wait_recv)
+    for late in range(2):
+        top, bottom = edall[2 * late].astype(F32), edall[2 * late + 1].astype(F32)
+        joined = [top[:, 96:], bottom[:, :160], jnp.zeros((48, 64), F32)]
+        joint[0, late] = jnp.concatenate(joined, axis=1).astype(BF16)
     for by in (1, 3, 2):
-        dy[by].append(send(edall.at[0], edall.at[by], shifted(at, y=by)))
+        dy[by].append(send(joint.at[0], joint.at[by], shifted(at, y=by)))
     column = lax.broadcasted_iota(jnp.int32, (CH, LANES), 1) % 160
     left_end, right_end = column == 0, column == 159
     next_on = jnp.where(at["x"] < 3, 1.0, 0.0).astype(F32)
@@ -153,14 +157,14 @@
                 own = dnall[slot].astype(F32)[rows]
             else:
                 own = (d_ref[...] if slot == 0 else dall[slot - 1]).astype(F32)[rows]
-            top = edall[slot, 2 if late else 0].astype(F32)[rows]
-            bottom = edall[slot, 3 if late else 1].astype(F32)[rows]
+            edge = joint[slot, tp // 2].astype(F32)[rows]
+            top, bottom = edge[:, :160], edge[:, 160:320]
             if late:
                 own, top, bottom = own * next_on, top * next_on, bottom * next_on
             moved = (
-                jnp.concatenate([own[:, 160:], bottom[:, :160]], axis=1),
+                jnp.concatenate([own[:, 160:], bottom], axis=1),
                 own,
-                jnp.concatenate([top[:, 96:], own[:, :480]], axis=1),
+                jnp.concatenate([top, own[:, :480]], axis=1),
             )
             pieces = []
             for one in moved:
@@ -445,7 +449,8 @@
             pltpu.VMEM((TOTAL, 8), F32),
             cells,
             pltpu.VMEM((4, 48, LANES), BF16),
-            pltpu.VMEM((4, 4, 48, 256), BF16),
+            pltpu.VMEM((4, 48, 256), BF16),
+            pltpu.VMEM((4, 2, 48, 384), BF16),
             pltpu.VMEM((4, 48, LANES), BF16),
             pltpu.VMEM((4, 4, 216, LANES), BF16),
             pltpu.VMEM((2, 96, LANES), F32),

time: 65.9 us -> 66 us (level)
  no operation moved by 1% of the time
where the time goes in v11:
time: 66 us; the launch traced here: 65.8 us
  Pallas kernels  61.5 us (93%)
  other arithmetic  2.17 us (3%)
  local copies, waits for them, and re-layouts  1.53 us (2%)
  between operations  0.7 us (1%)
    pallas_call x1, Pallas kernels, on_device(): pl.pallas_call(kernel, name='unit_backward', out_shape=(jax.ShapeDtypeStr...  61.5 us

profile of v11, /device:TPU:1, one launch (start us, length us, event | category | flops | bytes accessed | tf_op | source)
XLA Modules:
  0.0 65.8 jit_solution(12031422557196149149)
XLA Ops:
  0.6 0.0 copy-start
  0.6 1.2 %maximum_bitcast_fusion = bf16[2,2,24,4,160]{4,3,1,2,0:T(4,128)(2,1)S(1)} fusion(bf16[1,24,2,4,160]{4,3,2,1,0:T(4,128)(2,1)} %bitcast.17, bf16[1,24,2,4,160]{4,3,2,1,0:T(4,128)(2,1)} %bitcast.18), kind=kLoop, calls=%fused_computation.1 | loop fusion | flops 61440 | bytes 245760 | tf_op jit(solution)/shard_map/transpose | solution.py:425
  1.8 0.1 copy.7
  1.9 0.0 copy-start.1
  1.9 0.0 copy-start.2
  1.9 0.2 reshape.16.fd_ref
  2.1 0.0 copy-done
  2.1 0.5 copy-done.1
  2.6 0.0 copy-done.2
  2.6 61.5 %unit_backward.1 = (bf16[648,384]{1,0:T(8,128)(2,1)S(1)}, bf16[48,640]{1,0:T(8,128)(2,1)S(1)}) custom-call(bf16[96,640]{1,0:T(8,128)(2,1)S(1)} %reshape.16.fd_ref, bf16[648,384]{1,0:T(8,128)(2,1)S(1)} %bitcast.14, f32[384]{0:T(512)S(1)} %copy-done.1, f32[384]{0:T(512)S(1)} %copy-done.2), custom_call_target="tpu_custom_call" | custom-call | tf_op jit(solution)/shard_map/unit_backward/pallas_call | solution.py:433
  64.0 1.0 %convert_bitcast_fusion = f32[24,27,384]{2,0,1:T(8,128)} fusion(bf16[27,24,384]{2,1,0:T(8,128)(2,1)S(1)} %bitcast.15), kind=kLoop, calls=%fused_computation | loop fusion | flops 248832 | bytes 1492992 | tf_op jit(solution)/shard_map/convert_element_type | solution.py:486
  65.1 0.1 reshape.18
  65.2 0.7 %copy.10 = bf16[2,24,4,160]{3,2,0,1:T(4,128)(2,1)} copy(bf16[2,24,4,160]{3,2,1,0:T(4,128)(2,1)S(1)} %reshape.18) | data formatting | bytes 122880 | tf_op jit(solution)/shard_map/reshape | solution.py:485
Async XLA Ops:
  0.6 1.4 %copy-start = (bf16[24,27,384]{2,0,1:T(8,128)(2,1)S(1)}, bf16[24,27,384]{2,0,1:T(8,128)(2,1)}, u32[]{:S(2)}) copy-start(bf16[24,27,384]{2,0,1:T(8,128)(2,1)} %param.7) | copy-start | bytes 1492996
  1.9 0.7 %copy-start.1 = (f32[384]{0:T(512)S(1)}, f32[384]{0:T(512)}, u32[]{:S(2)}) copy-start(f32[384]{0:T(512)} %gain_hbm.1) | copy-start | bytes 4612
  1.9 0.7 %copy-start.2 = (f32[384]{0:T(512)S(1)}, f32[384]{0:T(512)}, u32[]{:S(2)}) copy-start(f32[384]{0:T(512)} %bias_hbm.1) | copy-start | bytes 4612

commit v12 on v10

--- a/solution.py
+++ b/solution.py
@@ -375,6 +375,8 @@
     arrived(a)
     a = core_gather(0)
 
+    arrived(b)
+    b = core_gather(2)
     arrived([z_near, z_sum] + dzs)
     grad = q[...] + rz[1].astype(F32) + rz[2].astype(F32)
     dots = dmid[...] + drz[0] + drz[1] + drz[2]
@@ -391,8 +393,6 @@
         outs.append(ct[rows] + back)
     od_ref[...] = jnp.concatenate(outs, axis=0).astype(BF16)
 
-    arrived(b)
-    b = core_gather(2)
     arrived([a])
     wgrad[...] = unpack(0) + unpack(1)
     arrived([b])

time: 65.9 us -> 65.9 us (level)
  no operation moved by 1% of the time
where the time goes in v12:
time: 65.9 us; the launch traced here: 65.8 us
  Pallas kernels  61.4 us (93%)
  other arithmetic  2.17 us (3%)
  local copies, waits for them, and re-layouts  1.53 us (2%)
  between operations  0.7 us (1%)
    pallas_call x1, Pallas kernels, on_device(): pl.pallas_call(kernel, name='unit_backward', out_shape=(jax.ShapeDtypeStr...  61.4 us

profile of v12, /device:TPU:1, one launch (start us, length us, event | category | flops | bytes accessed | tf_op | source)
XLA Modules:
  0.0 65.8 jit_solution(7857050539507065621)
XLA Ops:
  0.6 0.0 copy-start
  0.6 1.2 %maximum_bitcast_fusion = bf16[2,2,24,4,160]{4,3,1,2,0:T(4,128)(2,1)S(1)} fusion(bf16[1,24,2,4,160]{4,3,2,1,0:T(4,128)(2,1)} %bitcast.17, bf16[1,24,2,4,160]{4,3,2,1,0:T(4,128)(2,1)} %bitcast.18), kind=kLoop, calls=%fused_computation.1 | loop fusion | flops 61440 | bytes 245760 | tf_op jit(solution)/shard_map/transpose | solution.py:421
  1.8 0.1 copy.7
  1.9 0.0 copy-start.1
  1.9 0.0 copy-start.2
  1.9 0.2 reshape.16.fd_ref
  2.1 0.0 copy-done
  2.1 0.5 copy-done.1
  2.6 0.0 copy-done.2
  2.6 61.4 %unit_backward.1 = (bf16[648,384]{1,0:T(8,128)(2,1)S(1)}, bf16[48,640]{1,0:T(8,128)(2,1)S(1)}) custom-call(bf16[96,640]{1,0:T(8,128)(2,1)S(1)} %reshape.16.fd_ref, bf16[648,384]{1,0:T(8,128)(2,1)S(1)} %bitcast.14, f32[384]{0:T(512)S(1)} %copy-done.1, f32[384]{0:T(512)S(1)} %copy-done.2), custom_call_target="tpu_custom_call" | custom-call | tf_op jit(solution)/shard_map/unit_backward/pallas_call | solution.py:429
  64.0 1.0 %convert_bitcast_fusion = f32[24,27,384]{2,0,1:T(8,128)} fusion(bf16[27,24,384]{2,1,0:T(8,128)(2,1)S(1)} %bitcast.15), kind=kLoop, calls=%fused_computation | loop fusion | flops 248832 | bytes 1492992 | tf_op jit(solution)/shard_map/convert_element_type | solution.py:481
  65.0 0.1 reshape.18
  65.1 0.7 %copy.10 = bf16[2,24,4,160]{3,2,0,1:T(4,128)(2,1)} copy(bf16[2,24,4,160]{3,2,1,0:T(4,128)(2,1)S(1)} %reshape.18) | data formatting | bytes 122880 | tf_op jit(solution)/shard_map/reshape | solution.py:480
Async XLA Ops:
  0.6 1.4 %copy-start = (bf16[24,27,384]{2,0,1:T(8,128)(2,1)S(1)}, bf16[24,27,384]{2,0,1:T(8,128)(2,1)}, u32[]{:S(2)}) copy-start(bf16[24,27,384]{2,0,1:T(8,128)(2,1)} %param.7) | copy-start | bytes 1492996
  1.9 0.7 %copy-start.1 = (f32[384]{0:T(512)S(1)}, f32[384]{0:T(512)}, u32[]{:S(2)}) copy-start(f32[384]{0:T(512)} %gain_hbm.1) | copy-start | bytes 4612
  1.9 0.7 %copy-start.2 = (f32[384]{0:T(512)S(1)}, f32[384]{0:T(512)}, u32[]{:S(2)}) copy-start(f32[384]{0:T(512)} %bias_hbm.1) | copy-start | bytes 4612
